TPU v7x, 512 devices: a whole 4x8x8 slice. The times are simulated.
512 devices in a mesh: gx: 8 (over z), gy: 8 (over y_lo, core), gz: 8 (over x, y_hi).
Axes of the slice: x: 4, y: 8 (y_hi: 2, y_lo: 4; y = y_hi * 4 + y_lo), z: 8, core: 2. Of those that a mesh axis runs over, the one named last changes fastest.
Arguments:
- charges: float32 [128, 128, 1024], P('gx', 'gy', 'gz'), may hold values from -6 to 6
- exponents: float32 [2, 4], replicated, may hold values from 0.01 to 1
- amplitudes: float32 [2, 4], replicated, may hold values from 0.25 to 1
- top_x: float32 [8, 8], replicated, may hold values from -1 to 1
- top_y: float32 [8, 8], replicated, may hold values from -1 to 1
- top_z: float32 [64, 64], replicated, may hold values from -0.375 to 0.375
Outputs:
- potential: float32 [128, 128, 1024], P('gx', 'gy', 'gz')
All inputs are finite; a program needn't handle non-finite values.
Results may differ from a plain program's by a relative error of at most 0.0003.
Values sent between devices are 32-bit elements; how exact they have to be, the bound alone decides.
A program may use at most 64 MiB of HBM per device.

v0:
```python
import jax
import jax.numpy as jnp
from jax import lax
from jax.sharding import PartitionSpec as P

REACH = 8


HIGHEST = lax.Precision.HIGHEST


def with_halo(cells, sides, width):
    for axis, dim in sides:
        count = lax.axis_size(axis)
        head = lax.slice_in_dim(cells, 0, width, axis=dim)
        tail = lax.slice_in_dim(cells, cells.shape[dim] - width, cells.shape[dim], axis=dim)
        cells = jnp.concatenate(
            [
                lax.ppermute(tail, axis, [(i, (i + 1) % count) for i in range(count)]),
                cells,
                lax.ppermute(head, axis, [((i + 1) % count, i) for i in range(count)]),
            ],
            axis=dim,
        )
    return cells


def gauss_taps(exponents):
    offsets = jnp.arange(-REACH, REACH + 1).astype(jnp.float32)
    weights = jnp.exp(-exponents[..., None] * offsets * offsets)
    return weights / jnp.sum(weights, axis=-1, keepdims=True)


def spline(offsets):
    inner_weight = jnp.where((offsets == 1) | (offsets == 2), 0.75, 0.0)
    return jnp.where((offsets == 0) | (offsets == 3), 0.25, inner_weight).astype(jnp.float32)


def band_gauss(tap_table, length):
    rows = jnp.arange(length + 2 * REACH)[:, None]
    cols = jnp.arange(length)[None, :]
    offsets = rows - cols
    onehot = (offsets[:, :, None] == jnp.arange(2 * REACH + 1)[None, None, :]).astype(jnp.float32)
    return jnp.einsum("gk,pok->gpo", tap_table, onehot, precision=HIGHEST)


def band_restrict(length):
    rows = jnp.arange(length + 2)[:, None]
    cols = jnp.arange(length // 2)[None, :]
    return spline(rows - 2 * cols)


def band_prolong(length):
    rows = jnp.arange(length + 2)[:, None]
    cols = jnp.arange(2 * length)[None, :]
    return spline(cols - 2 * rows + 3)


def apply_three(field, band_x, band_y, band_z):
    field = jnp.einsum("xyz,zc->xyc", field, band_z, precision=HIGHEST)
    field = jnp.einsum("xyz,yb->xbz", field, band_y, precision=HIGHEST)
    return jnp.einsum("xyz,xa->ayz", field, band_x, precision=HIGHEST)


def rim_cells(field):
    return with_halo(field, (("gx", 0), ("gy", 1), ("gz", 2)), 1)


def restrict_local(padded):
    sizes = padded.shape
    return apply_three(
        padded,
        band_restrict(sizes[0] - 2),
        band_restrict(sizes[1] - 2),
        band_restrict(sizes[2] - 2),
    )


def prolong_local(field):
    sizes = field.shape
    return apply_three(
        rim_cells(field), band_prolong(sizes[0]), band_prolong(sizes[1]), band_prolong(sizes[2])
    )


def prolong_from_whole(whole_grid, brick):
    padded = jnp.pad(whole_grid, 1, mode="wrap")
    starts = (
        lax.axis_index("gx") * brick[0],
        lax.axis_index("gy") * brick[1],
        lax.axis_index("gz") * brick[2],
    )
    piece_cells = lax.dynamic_slice(padded, starts, (brick[0] + 2, brick[1] + 2, brick[2] + 2))
    return apply_three(
        piece_cells, band_prolong(brick[0]), band_prolong(brick[1]), band_prolong(brick[2])
    )


def assemble(gathered, brick):
    count_x = lax.axis_size("gx")
    count_y = lax.axis_size("gy")
    count_z = lax.axis_size("gz")
    blocks = gathered.reshape(count_x, count_y, count_z, brick[0], brick[1], brick[2])
    blocks = jnp.transpose(blocks, (0, 3, 1, 4, 2, 5))
    return blocks.reshape(count_x * brick[0], count_y * brick[1], count_z * brick[2])


def top_level(field, top_x, top_y, top_z):
    field = jnp.einsum("ia,abc->ibc", top_x, field, precision=HIGHEST)
    field = jnp.einsum("jb,ibc->ijc", top_y, field, precision=HIGHEST)
    return jnp.einsum("kc,ijc->ijk", top_z, field, precision=HIGHEST)


def gauss_and_restrict(field, tap_table, weights):
    size_x, size_y, size_z = field.shape
    band_z = band_gauss(tap_table, size_z)
    band_y = band_gauss(tap_table, size_y)
    band_x = band_gauss(tap_table, size_x) * weights[:, None, None]
    side_cells = with_halo(field, (("gz", 2),), REACH)
    along_z = jnp.einsum("xyp,gpo->xygo", side_cells, band_z, precision=HIGHEST)
    side_terms = with_halo(along_z, (("gy", 1),), REACH)
    along_y = jnp.einsum("xpgz,gpw->xgwz", side_terms, band_y, precision=HIGHEST)
    front_terms = with_halo(along_y, (("gx", 0),), REACH)
    result = jnp.einsum("pgwz,gpv->vwz", front_terms, band_x, precision=HIGHEST)
    coarse = restrict_local(rim_cells(field))
    return (result, coarse)


def local(charges, exponents, amplitudes, top_x, top_y, top_z):
    tap_table = gauss_taps(exponents)
    term_zero, level_one = gauss_and_restrict(charges, tap_table[0], amplitudes[0])
    term_one, level_two = gauss_and_restrict(level_one, tap_table[1], amplitudes[1])
    level_three = restrict_local(rim_cells(level_two))
    level_four = restrict_local(rim_cells(level_three))
    brick_four = level_four.shape
    gathered = lax.all_gather(level_four.reshape(1, -1), ("gx", "gy", "gz"), axis=0, tiled=True)
    phi_four = top_level(assemble(gathered, brick_four), top_x, top_y, top_z)
    phi_three = prolong_from_whole(phi_four, brick_four)
    phi_two = prolong_local(phi_three)
    phi_one = term_one + prolong_local(phi_two)
    return term_zero + prolong_local(phi_one)


def solution(mesh):
    in_specs = (P("gx", "gy", "gz"), P(), P(), P(), P(), P())
    out_specs = P("gx", "gy", "gz")
    return jax.shard_map(local, mesh=mesh, in_specs=in_specs, out_specs=out_specs, check_vma=False)
```

profile of v0, /device:TPU:1, one launch (start us, length us, event | category | flops | bytes accessed | tf_op | source)
XLA Modules:
  0.0 408.7 jit_solution(5014538539607518406)
XLA Ops:
  0.7 11.5 %collective-permute-start.7 = (f32[1,16,128]{2,1,0:T(8,128)S(1)}, f32[1,16,128]{2,1,0:T(8,128)S(1)}, u32[]{:S(2)}, u32[]{:S(2)}) collective-permute-start(f32[1,16,128]{2,1,0:T(8,128)S(1)} %get-tuple-element.15), channel_id=1, source_target_pairs={{64,0},{128,64},{192,128},{256,192},{320,256},{384,320},{448,384},... | collective-permute-start | bytes 24584 | tf_op jit(solution)/shard_map/ppermute | solution.py:21
  15.2 7.5 %collective-permute-start = (f32[16,16,8]{2,1,0:T(8,128)S(1)}, f32[16,16,8]{2,1,0:T(8,128)S(1)}, u32[]{:S(2)}, u32[]{:S(2)}) collective-permute-start(f32[16,16,8]{2,1,0:T(8,128)S(1)} %get-tuple-element.13), channel_id=1, source_target_pairs={{0,1},{1,2},{2,3},{3,4},{4,5},{5,6},{6,7},{7,0},{8,9},{9,10},{10,1... | collective-permute-start | bytes 24584 | tf_op jit(solution)/shard_map/ppermute | solution.py:19
  22.7 4.1 %collective-permute-start.1 = (f32[16,16,8]{2,1,0:T(8,128)S(1)}, f32[16,16,8]{2,1,0:T(8,128)S(1)}, u32[]{:S(2)}, u32[]{:S(2)}) collective-permute-start(f32[16,16,8]{2,1,0:T(8,128)S(1)} %get-tuple-element.14), channel_id=1, source_target_pairs={{1,0},{2,1},{3,2},{4,3},{5,4},{6,5},{7,6},{0,7},{9,8},{10,9},{11,1... | collective-permute-start | bytes 24584 | tf_op jit(solution)/shard_map/ppermute | solution.py:21
  30.5 4.3 %collective-permute-start.8 = (f32[18,1,128]{2,1,0:T(1,128)S(1)}, f32[18,1,128]{2,1,0:T(1,128)S(1)}, u32[]{:S(2)}, u32[]{:S(2)}) collective-permute-start(f32[18,1,128]{2,1,0:T(1,128)S(1)} %get-tuple-element.11), channel_id=1, source_target_pairs={{0,8},{8,16},{16,24},{24,32},{32,40},{40,48},{48,56},{56,0},{1,9},... | collective-permute-start | bytes 27656 | tf_op jit(solution)/shard_map/ppermute | solution.py:19
  36.8 3.0 collective-permute-done.9
  40.0 4.4 %collective-permute-start.10 = (f32[18,18,1]{2,1,0:T(8,128)S(1)}, f32[18,18,1]{2,1,0:T(8,128)S(1)}, u32[]{:S(2)}, u32[]{:S(2)}) collective-permute-start(f32[18,18,1]{2,1,0:T(8,128)S(1)} %get-tuple-element.9), channel_id=1, source_target_pairs={{0,1},{1,2},{2,3},{3,4},{4,5},{5,6},{6,7},{7,0},{8,9},{9,10},{10,1... | collective-permute-start | bytes 3896 | tf_op jit(solution)/shard_map/ppermute | solution.py:19
  44.5 6.9 %collective-permute-start.11 = (f32[18,18,1]{2,1,0:T(8,128)S(1)}, f32[18,18,1]{2,1,0:T(8,128)S(1)}, u32[]{:S(2)}, u32[]{:S(2)}) collective-permute-start(f32[18,18,1]{2,1,0:T(8,128)S(1)} %get-tuple-element.10), channel_id=1, source_target_pairs={{1,0},{2,1},{3,2},{4,3},{5,4},{6,5},{7,6},{0,7},{9,8},{10,9},{11,1... | collective-permute-start | bytes 3896 | tf_op jit(solution)/shard_map/ppermute | solution.py:21
  51.3 7.1 %collective-permute-done.10 = f32[18,18,1]{2,1,0:T(8,128)S(1)} collective-permute-done((f32[18,18,1]{2,1,0:T(8,128)S(1)}, f32[18,18,1]{2,1,0:T(8,128)S(1)}, u32[]{:S(2)}, u32[]{:S(2)}) %collective-permute-start.10) | collective-permute-done | bytes 1328 | tf_op jit(solution)/shard_map/ppermute | solution.py:19
  58.5 4.8 %collective-permute-done.11 = f32[18,18,1]{2,1,0:T(8,128)S(1)} collective-permute-done((f32[18,18,1]{2,1,0:T(8,128)S(1)}, f32[18,18,1]{2,1,0:T(8,128)S(1)}, u32[]{:S(2)}, u32[]{:S(2)}) %collective-permute-start.11) | collective-permute-done | bytes 1328 | tf_op jit(solution)/shard_map/ppermute | solution.py:21
  66.4 4.9 %collective-permute-start.19 = (f32[1,8,64]{2,0,1:T(1,128)S(1)}, f32[1,8,64]{2,0,1:T(1,128)S(1)}, u32[]{:S(2)}, u32[]{:S(2)}) collective-permute-start(f32[1,8,64]{2,0,1:T(1,128)S(1)} %get-tuple-element.36), channel_id=1, source_target_pairs={{64,0},{128,64},{192,128},{256,192},{320,256},{384,320},{448,384},... | collective-permute-start | bytes 6152 | tf_op jit(solution)/shard_map/ppermute | solution.py:21
  74.0 5.2 %collective-permute-start.21 = (f32[10,1,64]{2,0,1:T(8,128)S(1)}, f32[10,1,64]{2,0,1:T(8,128)S(1)}, u32[]{:S(2)}, u32[]{:S(2)}) collective-permute-start(f32[10,1,64]{2,0,1:T(8,128)S(1)} %get-tuple-element.28), channel_id=1, source_target_pairs={{8,0},{16,8},{24,16},{32,24},{40,32},{48,40},{56,48},{0,56},{9,1},... | collective-permute-start | bytes 7688 | tf_op jit(solution)/shard_map/ppermute | solution.py:21
  80.1 6.4 %collective-permute-start.22 = (f32[10,10,1]{2,0,1:T(8,128)S(1)}, f32[10,10,1]{2,0,1:T(8,128)S(1)}, u32[]{:S(2)}, u32[]{:S(2)}) collective-permute-start(f32[10,10,1]{2,0,1:T(8,128)S(1)} %get-tuple-element.21), channel_id=1, source_target_pairs={{0,1},{1,2},{2,3},{3,4},{4,5},{5,6},{6,7},{7,0},{8,9},{9,10},{10,1... | collective-permute-start | bytes 1208 | tf_op jit(solution)/shard_map/ppermute | solution.py:19
  86.6 4.9 %collective-permute-start.23 = (f32[10,10,1]{2,0,1:T(8,128)S(1)}, f32[10,10,1]{2,0,1:T(8,128)S(1)}, u32[]{:S(2)}, u32[]{:S(2)}) collective-permute-start(f32[10,10,1]{2,0,1:T(8,128)S(1)} %get-tuple-element.22), channel_id=1, source_target_pairs={{1,0},{2,1},{3,2},{4,3},{5,4},{6,5},{7,6},{0,7},{9,8},{10,9},{11,1... | collective-permute-start | bytes 1208 | tf_op jit(solution)/shard_map/ppermute | solution.py:21
  91.5 6.1 %collective-permute-done.23 = f32[10,10,1]{2,0,1:T(8,128)S(1)} collective-permute-done((f32[10,10,1]{2,0,1:T(8,128)S(1)}, f32[10,10,1]{2,0,1:T(8,128)S(1)}, u32[]{:S(2)}, u32[]{:S(2)}) %collective-permute-start.23) | collective-permute-done | bytes 432 | tf_op jit(solution)/shard_map/ppermute | solution.py:21
  100.4 5.1 %collective-permute-start.25 = (f32[1,4,32]{2,0,1:T(1,128)S(1)}, f32[1,4,32]{2,0,1:T(1,128)S(1)}, u32[]{:S(2)}, u32[]{:S(2)}) collective-permute-start(f32[1,4,32]{2,0,1:T(1,128)S(1)} %get-tuple-element.52), channel_id=1, source_target_pairs={{64,0},{128,64},{192,128},{256,192},{320,256},{384,320},{448,384},... | collective-permute-start | bytes 1544 | tf_op jit(solution)/shard_map/ppermute | solution.py:21
  106.3 6.0 %collective-permute-start.26 = (f32[6,1,32]{2,0,1:T(8,128)S(1)}, f32[6,1,32]{2,0,1:T(8,128)S(1)}, u32[]{:S(2)}, u32[]{:S(2)}) collective-permute-start(f32[6,1,32]{2,0,1:T(8,128)S(1)} %get-tuple-element.43), channel_id=1, source_target_pairs={{0,8},{8,16},{16,24},{24,32},{32,40},{40,48},{48,56},{56,0},{1,9},... | collective-permute-start | bytes 2312 | tf_op jit(solution)/shard_map/ppermute | solution.py:19
  114.3 3.0 collective-permute-done.27
  117.3 4.7 %collective-permute-start.28 = (f32[6,6,1]{2,0,1:T(8,128)S(1)}, f32[6,6,1]{2,0,1:T(8,128)S(1)}, u32[]{:S(2)}, u32[]{:S(2)}) collective-permute-start(f32[6,6,1]{2,0,1:T(8,128)S(1)} %get-tuple-element.39), channel_id=1, source_target_pairs={{0,1},{1,2},{2,3},{3,4},{4,5},{5,6},{6,7},{7,0},{8,9},{9,10},{10,1... | collective-permute-start | bytes 440 | tf_op jit(solution)/shard_map/ppermute | solution.py:19
  122.0 6.6 %collective-permute-start.29 = (f32[6,6,1]{2,0,1:T(8,128)S(1)}, f32[6,6,1]{2,0,1:T(8,128)S(1)}, u32[]{:S(2)}, u32[]{:S(2)}) collective-permute-start(f32[6,6,1]{2,0,1:T(8,128)S(1)} %get-tuple-element.40), channel_id=1, source_target_pairs={{1,0},{2,1},{3,2},{4,3},{5,4},{6,5},{7,6},{0,7},{9,8},{10,9},{11,1... | collective-permute-start | bytes 440 | tf_op jit(solution)/shard_map/ppermute | solution.py:21
  131.3 2.3 collective-permute-start.30
  133.6 4.7 %collective-permute-start.31 = (f32[1,2,16]{2,0,1:T(1,128)S(1)}, f32[1,2,16]{2,0,1:T(1,128)S(1)}, u32[]{:S(2)}, u32[]{:S(2)}) collective-permute-start(f32[1,2,16]{2,0,1:T(1,128)S(1)} %get-tuple-element.60), channel_id=1, source_target_pairs={{64,0},{128,64},{192,128},{256,192},{320,256},{384,320},{448,384},... | collective-permute-start | bytes 392 | tf_op jit(solution)/shard_map/ppermute | solution.py:21
  139.1 5.0 %collective-permute-start.32 = (f32[4,1,16]{2,0,1:T(4,128)S(1)}, f32[4,1,16]{2,0,1:T(4,128)S(1)}, u32[]{:S(2)}, u32[]{:S(2)}) collective-permute-start(f32[4,1,16]{2,0,1:T(4,128)S(1)} %get-tuple-element.55), channel_id=1, source_target_pairs={{0,8},{8,16},{16,24},{24,32},{32,40},{40,48},{48,56},{56,0},{1,9},... | collective-permute-start | bytes 776 | tf_op jit(solution)/shard_map/ppermute | solution.py:19
  144.1 3.2 collective-permute-start.33
  149.4 4.7 %collective-permute-start.34 = (f32[4,4,1]{2,0,1:T(4,128)S(1)}, f32[4,4,1]{2,0,1:T(4,128)S(1)}, u32[]{:S(2)}, u32[]{:S(2)}) collective-permute-start(f32[4,4,1]{2,0,1:T(4,128)S(1)} %get-tuple-element.49), channel_id=1, source_target_pairs={{0,1},{1,2},{2,3},{3,4},{4,5},{5,6},{6,7},{7,0},{8,9},{9,10},{10,1... | collective-permute-start | bytes 200 | tf_op jit(solution)/shard_map/ppermute | solution.py:19
  154.1 6.5 %collective-permute-start.35 = (f32[4,4,1]{2,0,1:T(4,128)S(1)}, f32[4,4,1]{2,0,1:T(4,128)S(1)}, u32[]{:S(2)}, u32[]{:S(2)}) collective-permute-start(f32[4,4,1]{2,0,1:T(4,128)S(1)} %get-tuple-element.50), channel_id=1, source_target_pairs={{1,0},{2,1},{3,2},{4,3},{5,4},{6,5},{7,6},{0,7},{9,8},{10,9},{11,1... | collective-permute-start | bytes 200 | tf_op jit(solution)/shard_map/ppermute | solution.py:21
  163.6 103.7 %all-reduce = f32[4096]{0:T(1024)S(1)} all-reduce(f32[4096]{0:T(1024)S(1)} %dynamic-update-slice), channel_id=2, replica_groups=mesh['gx'=8,'gy'=8,'gz'=8] {'gx','gy','gz'}, use_global_device_ids=true, to_apply=%add | all-reduce | flops 4096 | bytes 32768
  270.6 4.6 %collective-permute-start.37 = (f32[1,2,16]{2,0,1:T(1,128)S(1)}, f32[1,2,16]{2,0,1:T(1,128)S(1)}, u32[]{:S(2)}, u32[]{:S(2)}) collective-permute-start(f32[1,2,16]{2,0,1:T(1,128)S(1)} %get-tuple-element.58), channel_id=1, source_target_pairs={{64,0},{128,64},{192,128},{256,192},{320,256},{384,320},{448,384},... | collective-permute-start | bytes 392 | tf_op jit(solution)/shard_map/ppermute | solution.py:21
  275.9 3.1 collective-permute-start.38
  279.0 2.5 collective-permute-start.39
  281.6 3.9 collective-permute-start.12
  285.6 6.6 %collective-permute-start.40 = (f32[4,4,1]{2,0,1:T(4,128)S(1)}, f32[4,4,1]{2,0,1:T(4,128)S(1)}, u32[]{:S(2)}, u32[]{:S(2)}) collective-permute-start(f32[4,4,1]{2,0,1:T(4,128)S(1)} %get-tuple-element.47), channel_id=1, source_target_pairs={{0,1},{1,2},{2,3},{3,4},{4,5},{5,6},{6,7},{7,0},{8,9},{9,10},{10,1... | collective-permute-start | bytes 200 | tf_op jit(solution)/shard_map/ppermute | solution.py:19
  292.2 4.7 %collective-permute-start.41 = (f32[4,4,1]{2,0,1:T(4,128)S(1)}, f32[4,4,1]{2,0,1:T(4,128)S(1)}, u32[]{:S(2)}, u32[]{:S(2)}) collective-permute-start(f32[4,4,1]{2,0,1:T(4,128)S(1)} %get-tuple-element.48), channel_id=1, source_target_pairs={{1,0},{2,1},{3,2},{4,3},{5,4},{6,5},{7,6},{0,7},{9,8},{10,9},{11,1... | collective-permute-start | bytes 200 | tf_op jit(solution)/shard_map/ppermute | solution.py:21
  296.9 5.3 %collective-permute-start.13 = (f32[8,8,8]{2,0,1:T(8,128)S(1)}, f32[8,8,8]{2,0,1:T(8,128)S(1)}, u32[]{:S(2)}, u32[]{:S(2)}) collective-permute-start(f32[8,8,8]{2,0,1:T(8,128)S(1)} %get-tuple-element.32), channel_id=1, source_target_pairs={{1,0},{2,1},{3,2},{4,3},{5,4},{6,5},{7,6},{0,7},{9,8},{10,9},{11,1... | collective-permute-start | bytes 6152 | tf_op jit(solution)/shard_map/ppermute | solution.py:21
  305.2 4.7 %collective-permute-start.43 = (f32[1,4,32]{2,0,1:T(1,128)S(1)}, f32[1,4,32]{2,0,1:T(1,128)S(1)}, u32[]{:S(2)}, u32[]{:S(2)}) collective-permute-start(f32[1,4,32]{2,0,1:T(1,128)S(1)} %get-tuple-element.46), channel_id=1, source_target_pairs={{64,0},{128,64},{192,128},{256,192},{320,256},{384,320},{448,384},... | collective-permute-start | bytes 1544 | tf_op jit(solution)/shard_map/ppermute | solution.py:21
  310.7 4.8 %collective-permute-start.44 = (f32[6,1,32]{2,0,1:T(8,128)S(1)}, f32[6,1,32]{2,0,1:T(8,128)S(1)}, u32[]{:S(2)}, u32[]{:S(2)}) collective-permute-start(f32[6,1,32]{2,0,1:T(8,128)S(1)} %get-tuple-element.41), channel_id=1, source_target_pairs={{0,8},{8,16},{16,24},{24,32},{32,40},{40,48},{48,56},{56,0},{1,9},... | collective-permute-start | bytes 2312 | tf_op jit(solution)/shard_map/ppermute | solution.py:19
  315.4 4.6 %collective-permute-start.45 = (f32[6,1,32]{2,0,1:T(8,128)S(1)}, f32[6,1,32]{2,0,1:T(8,128)S(1)}, u32[]{:S(2)}, u32[]{:S(2)}) collective-permute-start(f32[6,1,32]{2,0,1:T(8,128)S(1)} %get-tuple-element.42), channel_id=1, source_target_pairs={{8,0},{16,8},{24,16},{32,24},{40,32},{48,40},{56,48},{0,56},{9,1},... | collective-permute-start | bytes 2312 | tf_op jit(solution)/shard_map/ppermute | solution.py:21
  320.5 5.4 %collective-permute-start.15 = (f32[8,8,4,64]{3,1,2,0:T(8,128)S(1)}, f32[8,8,4,64]{3,1,2,0:T(8,128)S(1)}, u32[]{:S(2)}, u32[]{:S(2)}) collective-permute-start(f32[8,8,4,64]{3,1,2,0:T(8,128)S(1)} %fusion.28), channel_id=1, source_target_pairs={{8,0},{16,8},{24,16},{32,24},{40,32},{48,40},{56,48},{0,56},{9,1},... | collective-permute-start | bytes 196616 | tf_op jit(solution)/shard_map/ppermute | solution.py:21
  326.1 3.8 collective-permute-start.46
  329.9 7.4 %collective-permute-start.47 = (f32[6,6,1]{2,0,1:T(8,128)S(1)}, f32[6,6,1]{2,0,1:T(8,128)S(1)}, u32[]{:S(2)}, u32[]{:S(2)}) collective-permute-start(f32[6,6,1]{2,0,1:T(8,128)S(1)} %get-tuple-element.38), channel_id=1, source_target_pairs={{1,0},{2,1},{3,2},{4,3},{5,4},{6,5},{7,6},{0,7},{9,8},{10,9},{11,1... | collective-permute-start | bytes 440 | tf_op jit(solution)/shard_map/ppermute | solution.py:21
  341.6 5.1 %collective-permute-start.17 = (f32[8,4,8,64]{3,2,0,1:T(8,128)S(1)}, f32[8,4,8,64]{3,2,0,1:T(8,128)S(1)}, u32[]{:S(2)}, u32[]{:S(2)}) collective-permute-start(f32[8,4,8,64]{3,2,0,1:T(8,128)S(1)} %convolution_bitcast_fusion.1), channel_id=1, source_target_pairs={{64,0},{128,64},{192,128},{256,192},{320,256},{384,320},{448,384},... | collective-permute-start | bytes 196616 | tf_op jit(solution)/shard_map/ppermute | solution.py:21
  348.8 4.8 %collective-permute-done.16 = f32[8,4,8,64]{3,2,0,1:T(8,128)S(1)} collective-permute-done((f32[8,4,8,64]{3,2,0,1:T(8,128)S(1)}, f32[8,4,8,64]{3,2,0,1:T(8,128)S(1)}, u32[]{:S(2)}, u32[]{:S(2)}) %collective-permute-start.16) | collective-permute-done | bytes 65568 | tf_op jit(solution)/shard_map/ppermute | solution.py:19
  356.1 4.6 %collective-permute-start.49 = (f32[1,8,64]{2,0,1:T(1,128)S(1)}, f32[1,8,64]{2,0,1:T(1,128)S(1)}, u32[]{:S(2)}, u32[]{:S(2)}) collective-permute-start(f32[1,8,64]{2,0,1:T(1,128)S(1)} %get-tuple-element.30), channel_id=1, source_target_pairs={{64,0},{128,64},{192,128},{256,192},{320,256},{384,320},{448,384},... | collective-permute-start | bytes 6152 | tf_op jit(solution)/shard_map/ppermute | solution.py:21
  361.4 6.9 %collective-permute-start.50 = (f32[10,1,64]{2,0,1:T(8,128)S(1)}, f32[10,1,64]{2,0,1:T(8,128)S(1)}, u32[]{:S(2)}, u32[]{:S(2)}) collective-permute-start(f32[10,1,64]{2,0,1:T(8,128)S(1)} %get-tuple-element.23), channel_id=1, source_target_pairs={{0,8},{8,16},{16,24},{24,32},{32,40},{40,48},{48,56},{56,0},{1,9},... | collective-permute-start | bytes 7688 | tf_op jit(solution)/shard_map/ppermute | solution.py:19
  368.3 4.3 %collective-permute-start.51 = (f32[10,1,64]{2,0,1:T(8,128)S(1)}, f32[10,1,64]{2,0,1:T(8,128)S(1)}, u32[]{:S(2)}, u32[]{:S(2)}) collective-permute-start(f32[10,1,64]{2,0,1:T(8,128)S(1)} %get-tuple-element.24), channel_id=1, source_target_pairs={{8,0},{16,8},{24,16},{32,24},{40,32},{48,40},{56,48},{0,56},{9,1},... | collective-permute-start | bytes 7688 | tf_op jit(solution)/shard_map/ppermute | solution.py:21
  375.5 9.4 %collective-permute-start.53 = (f32[10,10,1]{2,0,1:T(8,128)S(1)}, f32[10,10,1]{2,0,1:T(8,128)S(1)}, u32[]{:S(2)}, u32[]{:S(2)}) collective-permute-start(f32[10,10,1]{2,0,1:T(8,128)S(1)} %get-tuple-element.18), channel_id=1, source_target_pairs={{1,0},{2,1},{3,2},{4,3},{5,4},{6,5},{7,6},{0,7},{9,8},{10,9},{11,1... | collective-permute-start | bytes 1208 | tf_op jit(solution)/shard_map/ppermute | solution.py:21
  384.9 2.4 collective-permute-start.2
  387.3 6.1 %collective-permute-start.3 = (f32[16,8,4,128]{3,1,2,0:T(8,128)S(1)}, f32[16,8,4,128]{3,1,2,0:T(8,128)S(1)}, u32[]{:S(2)}, u32[]{:S(2)}) collective-permute-start(f32[16,8,4,128]{3,1,2,0:T(8,128)S(1)} %get-tuple-element.8), channel_id=1, source_target_pairs={{8,0},{16,8},{24,16},{32,24},{40,32},{48,40},{56,48},{0,56},{9,1},... | collective-permute-start | bytes 786440 | tf_op jit(solution)/shard_map/ppermute | solution.py:21
  398.5 5.1 %collective-permute-start.5 = (f32[8,4,16,128]{3,2,0,1:T(8,128)S(1)}, f32[8,4,16,128]{3,2,0,1:T(8,128)S(1)}, u32[]{:S(2)}, u32[]{:S(2)}) collective-permute-start(f32[8,4,16,128]{3,2,0,1:T(8,128)S(1)} %get-tuple-element.6), channel_id=1, source_target_pairs={{64,0},{128,64},{192,128},{256,192},{320,256},{384,320},{448,384},... | collective-permute-start | bytes 786440 | tf_op jit(solution)/shard_map/ppermute | solution.py:21
  (183 shorter events, 60.5 us)
Async XLA Ops:
  0.7 29.8 %collective-permute-start.7 = (f32[1,16,128]{2,1,0:T(8,128)S(1)}, f32[1,16,128]{2,1,0:T(8,128)S(1)}, u32[]{:S(2)}, u32[]{:S(2)}) collective-permute-start(f32[1,16,128]{2,1,0:T(8,128)S(1)} %get-tuple-element.15), channel_id=1, source_target_pairs={{64,0},{128,64},{192,128},{256,192},{320,256},{384,320},{448,384},... | collective-permute-start | bytes 24584 | tf_op jit(solution)/shard_map/ppermute | solution.py:21
  12.2 18.2 %collective-permute-start.6 = (f32[1,16,128]{2,1,0:T(8,128)S(1)}, f32[1,16,128]{2,1,0:T(8,128)S(1)}, u32[]{:S(2)}, u32[]{:S(2)}) collective-permute-start(f32[1,16,128]{2,1,0:T(8,128)S(1)} %get-tuple-element.16), channel_id=1, source_target_pairs={{0,64},{64,128},{128,192},{192,256},{256,320},{320,384},{384,448},... | collective-permute-start | bytes 24584 | tf_op jit(solution)/shard_map/ppermute | solution.py:19
  15.2 357.4 %collective-permute-start = (f32[16,16,8]{2,1,0:T(8,128)S(1)}, f32[16,16,8]{2,1,0:T(8,128)S(1)}, u32[]{:S(2)}, u32[]{:S(2)}) collective-permute-start(f32[16,16,8]{2,1,0:T(8,128)S(1)} %get-tuple-element.13), channel_id=1, source_target_pairs={{0,1},{1,2},{2,3},{3,4},{4,5},{5,6},{6,7},{7,0},{8,9},{9,10},{10,1... | collective-permute-start | bytes 24584 | tf_op jit(solution)/shard_map/ppermute | solution.py:19
  22.7 349.9 %collective-permute-start.1 = (f32[16,16,8]{2,1,0:T(8,128)S(1)}, f32[16,16,8]{2,1,0:T(8,128)S(1)}, u32[]{:S(2)}, u32[]{:S(2)}) collective-permute-start(f32[16,16,8]{2,1,0:T(8,128)S(1)} %get-tuple-element.14), channel_id=1, source_target_pairs={{1,0},{2,1},{3,2},{4,3},{5,4},{6,5},{7,6},{0,7},{9,8},{10,9},{11,1... | collective-permute-start | bytes 24584 | tf_op jit(solution)/shard_map/ppermute | solution.py:21
  30.5 6.3 %collective-permute-start.8 = (f32[18,1,128]{2,1,0:T(1,128)S(1)}, f32[18,1,128]{2,1,0:T(1,128)S(1)}, u32[]{:S(2)}, u32[]{:S(2)}) collective-permute-start(f32[18,1,128]{2,1,0:T(1,128)S(1)} %get-tuple-element.11), channel_id=1, source_target_pairs={{0,8},{8,16},{16,24},{24,32},{32,40},{40,48},{48,56},{56,0},{1,9},... | collective-permute-start | bytes 27656 | tf_op jit(solution)/shard_map/ppermute | solution.py:19
  40.0 18.4 %collective-permute-start.10 = (f32[18,18,1]{2,1,0:T(8,128)S(1)}, f32[18,18,1]{2,1,0:T(8,128)S(1)}, u32[]{:S(2)}, u32[]{:S(2)}) collective-permute-start(f32[18,18,1]{2,1,0:T(8,128)S(1)} %get-tuple-element.9), channel_id=1, source_target_pairs={{0,1},{1,2},{2,3},{3,4},{4,5},{5,6},{6,7},{7,0},{8,9},{9,10},{10,1... | collective-permute-start | bytes 3896 | tf_op jit(solution)/shard_map/ppermute | solution.py:19
  44.5 18.8 %collective-permute-start.11 = (f32[18,18,1]{2,1,0:T(8,128)S(1)}, f32[18,18,1]{2,1,0:T(8,128)S(1)}, u32[]{:S(2)}, u32[]{:S(2)}) collective-permute-start(f32[18,18,1]{2,1,0:T(8,128)S(1)} %get-tuple-element.10), channel_id=1, source_target_pairs={{1,0},{2,1},{3,2},{4,3},{5,4},{6,5},{7,6},{0,7},{9,8},{10,9},{11,1... | collective-permute-start | bytes 3896 | tf_op jit(solution)/shard_map/ppermute | solution.py:21
  64.5 6.8 %collective-permute-start.18 = (f32[1,8,64]{2,0,1:T(1,128)S(1)}, f32[1,8,64]{2,0,1:T(1,128)S(1)}, u32[]{:S(2)}, u32[]{:S(2)}) collective-permute-start(f32[1,8,64]{2,0,1:T(1,128)S(1)} %get-tuple-element.35), channel_id=1, source_target_pairs={{0,64},{64,128},{128,192},{192,256},{256,320},{320,384},{384,448},... | collective-permute-start | bytes 6152 | tf_op jit(solution)/shard_map/ppermute | solution.py:19
  66.4 5.6 %collective-permute-start.19 = (f32[1,8,64]{2,0,1:T(1,128)S(1)}, f32[1,8,64]{2,0,1:T(1,128)S(1)}, u32[]{:S(2)}, u32[]{:S(2)}) collective-permute-start(f32[1,8,64]{2,0,1:T(1,128)S(1)} %get-tuple-element.36), channel_id=1, source_target_pairs={{64,0},{128,64},{192,128},{256,192},{320,256},{384,320},{448,384},... | collective-permute-start | bytes 6152 | tf_op jit(solution)/shard_map/ppermute | solution.py:21
  72.1 7.2 %collective-permute-start.20 = (f32[10,1,64]{2,0,1:T(8,128)S(1)}, f32[10,1,64]{2,0,1:T(8,128)S(1)}, u32[]{:S(2)}, u32[]{:S(2)}) collective-permute-start(f32[10,1,64]{2,0,1:T(8,128)S(1)} %get-tuple-element.27), channel_id=1, source_target_pairs={{0,8},{8,16},{16,24},{24,32},{32,40},{40,48},{48,56},{56,0},{1,9},... | collective-permute-start | bytes 7688 | tf_op jit(solution)/shard_map/ppermute | solution.py:19
  74.0 6.0 %collective-permute-start.21 = (f32[10,1,64]{2,0,1:T(8,128)S(1)}, f32[10,1,64]{2,0,1:T(8,128)S(1)}, u32[]{:S(2)}, u32[]{:S(2)}) collective-permute-start(f32[10,1,64]{2,0,1:T(8,128)S(1)} %get-tuple-element.28), channel_id=1, source_target_pairs={{8,0},{16,8},{24,16},{32,24},{40,32},{48,40},{56,48},{0,56},{9,1},... | collective-permute-start | bytes 7688 | tf_op jit(solution)/shard_map/ppermute | solution.py:21
  80.1 11.3 %collective-permute-start.22 = (f32[10,10,1]{2,0,1:T(8,128)S(1)}, f32[10,10,1]{2,0,1:T(8,128)S(1)}, u32[]{:S(2)}, u32[]{:S(2)}) collective-permute-start(f32[10,10,1]{2,0,1:T(8,128)S(1)} %get-tuple-element.21), channel_id=1, source_target_pairs={{0,1},{1,2},{2,3},{3,4},{4,5},{5,6},{6,7},{7,0},{8,9},{9,10},{10,1... | collective-permute-start | bytes 1208 | tf_op jit(solution)/shard_map/ppermute | solution.py:19
  86.6 11.0 %collective-permute-start.23 = (f32[10,10,1]{2,0,1:T(8,128)S(1)}, f32[10,10,1]{2,0,1:T(8,128)S(1)}, u32[]{:S(2)}, u32[]{:S(2)}) collective-permute-start(f32[10,10,1]{2,0,1:T(8,128)S(1)} %get-tuple-element.22), channel_id=1, source_target_pairs={{1,0},{2,1},{3,2},{4,3},{5,4},{6,5},{7,6},{0,7},{9,8},{10,9},{11,1... | collective-permute-start | bytes 1208 | tf_op jit(solution)/shard_map/ppermute | solution.py:21
  98.5 7.1 %collective-permute-start.24 = (f32[1,4,32]{2,0,1:T(1,128)S(1)}, f32[1,4,32]{2,0,1:T(1,128)S(1)}, u32[]{:S(2)}, u32[]{:S(2)}) collective-permute-start(f32[1,4,32]{2,0,1:T(1,128)S(1)} %get-tuple-element.51), channel_id=1, source_target_pairs={{0,64},{64,128},{128,192},{192,256},{256,320},{320,384},{384,448},... | collective-permute-start | bytes 1544 | tf_op jit(solution)/shard_map/ppermute | solution.py:19
  100.4 5.8 %collective-permute-start.25 = (f32[1,4,32]{2,0,1:T(1,128)S(1)}, f32[1,4,32]{2,0,1:T(1,128)S(1)}, u32[]{:S(2)}, u32[]{:S(2)}) collective-permute-start(f32[1,4,32]{2,0,1:T(1,128)S(1)} %get-tuple-element.52), channel_id=1, source_target_pairs={{64,0},{128,64},{192,128},{256,192},{320,256},{384,320},{448,384},... | collective-permute-start | bytes 1544 | tf_op jit(solution)/shard_map/ppermute | solution.py:21
  106.3 8.0 %collective-permute-start.26 = (f32[6,1,32]{2,0,1:T(8,128)S(1)}, f32[6,1,32]{2,0,1:T(8,128)S(1)}, u32[]{:S(2)}, u32[]{:S(2)}) collective-permute-start(f32[6,1,32]{2,0,1:T(8,128)S(1)} %get-tuple-element.43), channel_id=1, source_target_pairs={{0,8},{8,16},{16,24},{24,32},{32,40},{40,48},{48,56},{56,0},{1,9},... | collective-permute-start | bytes 2312 | tf_op jit(solution)/shard_map/ppermute | solution.py:19
  117.3 11.3 %collective-permute-start.28 = (f32[6,6,1]{2,0,1:T(8,128)S(1)}, f32[6,6,1]{2,0,1:T(8,128)S(1)}, u32[]{:S(2)}, u32[]{:S(2)}) collective-permute-start(f32[6,6,1]{2,0,1:T(8,128)S(1)} %get-tuple-element.39), channel_id=1, source_target_pairs={{0,1},{1,2},{2,3},{3,4},{4,5},{5,6},{6,7},{7,0},{8,9},{9,10},{10,1... | collective-permute-start | bytes 440 | tf_op jit(solution)/shard_map/ppermute | solution.py:19
  122.0 8.5 %collective-permute-start.29 = (f32[6,6,1]{2,0,1:T(8,128)S(1)}, f32[6,6,1]{2,0,1:T(8,128)S(1)}, u32[]{:S(2)}, u32[]{:S(2)}) collective-permute-start(f32[6,6,1]{2,0,1:T(8,128)S(1)} %get-tuple-element.40), channel_id=1, source_target_pairs={{1,0},{2,1},{3,2},{4,3},{5,4},{6,5},{7,6},{0,7},{9,8},{10,9},{11,1... | collective-permute-start | bytes 440 | tf_op jit(solution)/shard_map/ppermute | solution.py:21
  131.3 7.1 %collective-permute-start.30 = (f32[1,2,16]{2,0,1:T(1,128)S(1)}, f32[1,2,16]{2,0,1:T(1,128)S(1)}, u32[]{:S(2)}, u32[]{:S(2)}) collective-permute-start(f32[1,2,16]{2,0,1:T(1,128)S(1)} %get-tuple-element.59), channel_id=1, source_target_pairs={{0,64},{64,128},{128,192},{192,256},{256,320},{320,384},{384,448},... | collective-permute-start | bytes 392 | tf_op jit(solution)/shard_map/ppermute | solution.py:19
  133.6 5.4 %collective-permute-start.31 = (f32[1,2,16]{2,0,1:T(1,128)S(1)}, f32[1,2,16]{2,0,1:T(1,128)S(1)}, u32[]{:S(2)}, u32[]{:S(2)}) collective-permute-start(f32[1,2,16]{2,0,1:T(1,128)S(1)} %get-tuple-element.60), channel_id=1, source_target_pairs={{64,0},{128,64},{192,128},{256,192},{320,256},{384,320},{448,384},... | collective-permute-start | bytes 392 | tf_op jit(solution)/shard_map/ppermute | solution.py:21
  139.1 8.2 %collective-permute-start.32 = (f32[4,1,16]{2,0,1:T(4,128)S(1)}, f32[4,1,16]{2,0,1:T(4,128)S(1)}, u32[]{:S(2)}, u32[]{:S(2)}) collective-permute-start(f32[4,1,16]{2,0,1:T(4,128)S(1)} %get-tuple-element.55), channel_id=1, source_target_pairs={{0,8},{8,16},{16,24},{24,32},{32,40},{40,48},{48,56},{56,0},{1,9},... | collective-permute-start | bytes 776 | tf_op jit(solution)/shard_map/ppermute | solution.py:19
  149.4 11.3 %collective-permute-start.34 = (f32[4,4,1]{2,0,1:T(4,128)S(1)}, f32[4,4,1]{2,0,1:T(4,128)S(1)}, u32[]{:S(2)}, u32[]{:S(2)}) collective-permute-start(f32[4,4,1]{2,0,1:T(4,128)S(1)} %get-tuple-element.49), channel_id=1, source_target_pairs={{0,1},{1,2},{2,3},{3,4},{4,5},{5,6},{6,7},{7,0},{8,9},{9,10},{10,1... | collective-permute-start | bytes 200 | tf_op jit(solution)/shard_map/ppermute | solution.py:19
  154.1 8.6 %collective-permute-start.35 = (f32[4,4,1]{2,0,1:T(4,128)S(1)}, f32[4,4,1]{2,0,1:T(4,128)S(1)}, u32[]{:S(2)}, u32[]{:S(2)}) collective-permute-start(f32[4,4,1]{2,0,1:T(4,128)S(1)} %get-tuple-element.50), channel_id=1, source_target_pairs={{1,0},{2,1},{3,2},{4,3},{5,4},{6,5},{7,6},{0,7},{9,8},{10,9},{11,1... | collective-permute-start | bytes 200 | tf_op jit(solution)/shard_map/ppermute | solution.py:21
  268.7 6.5 %collective-permute-start.36 = (f32[1,2,16]{2,0,1:T(1,128)S(1)}, f32[1,2,16]{2,0,1:T(1,128)S(1)}, u32[]{:S(2)}, u32[]{:S(2)}) collective-permute-start(f32[1,2,16]{2,0,1:T(1,128)S(1)} %get-tuple-element.57), channel_id=1, source_target_pairs={{0,64},{64,128},{128,192},{192,256},{256,320},{320,384},{384,448},... | collective-permute-start | bytes 392 | tf_op jit(solution)/shard_map/ppermute | solution.py:19
  275.9 9.6 %collective-permute-start.38 = (f32[4,1,16]{2,0,1:T(4,128)S(1)}, f32[4,1,16]{2,0,1:T(4,128)S(1)}, u32[]{:S(2)}, u32[]{:S(2)}) collective-permute-start(f32[4,1,16]{2,0,1:T(4,128)S(1)} %get-tuple-element.53), channel_id=1, source_target_pairs={{0,8},{8,16},{16,24},{24,32},{32,40},{40,48},{48,56},{56,0},{1,9},... | collective-permute-start | bytes 776 | tf_op jit(solution)/shard_map/ppermute | solution.py:19
  279.0 6.5 %collective-permute-start.39 = (f32[4,1,16]{2,0,1:T(4,128)S(1)}, f32[4,1,16]{2,0,1:T(4,128)S(1)}, u32[]{:S(2)}, u32[]{:S(2)}) collective-permute-start(f32[4,1,16]{2,0,1:T(4,128)S(1)} %get-tuple-element.54), channel_id=1, source_target_pairs={{8,0},{16,8},{24,16},{32,24},{40,32},{48,40},{56,48},{0,56},{9,1},... | collective-permute-start | bytes 776 | tf_op jit(solution)/shard_map/ppermute | solution.py:21
  281.6 23.6 %collective-permute-start.12 = (f32[8,8,8]{2,0,1:T(8,128)S(1)}, f32[8,8,8]{2,0,1:T(8,128)S(1)}, u32[]{:S(2)}, u32[]{:S(2)}) collective-permute-start(f32[8,8,8]{2,0,1:T(8,128)S(1)} %get-tuple-element.31), channel_id=1, source_target_pairs={{0,1},{1,2},{2,3},{3,4},{4,5},{5,6},{6,7},{7,0},{8,9},{9,10},{10,1... | collective-permute-start | bytes 6152 | tf_op jit(solution)/shard_map/ppermute | solution.py:19
  285.6 11.3 %collective-permute-start.40 = (f32[4,4,1]{2,0,1:T(4,128)S(1)}, f32[4,4,1]{2,0,1:T(4,128)S(1)}, u32[]{:S(2)}, u32[]{:S(2)}) collective-permute-start(f32[4,4,1]{2,0,1:T(4,128)S(1)} %get-tuple-element.47), channel_id=1, source_target_pairs={{0,1},{1,2},{2,3},{3,4},{4,5},{5,6},{6,7},{7,0},{8,9},{9,10},{10,1... | collective-permute-start | bytes 200 | tf_op jit(solution)/shard_map/ppermute | solution.py:19
  292.2 10.1 %collective-permute-start.41 = (f32[4,4,1]{2,0,1:T(4,128)S(1)}, f32[4,4,1]{2,0,1:T(4,128)S(1)}, u32[]{:S(2)}, u32[]{:S(2)}) collective-permute-start(f32[4,4,1]{2,0,1:T(4,128)S(1)} %get-tuple-element.48), channel_id=1, source_target_pairs={{1,0},{2,1},{3,2},{4,3},{5,4},{6,5},{7,6},{0,7},{9,8},{10,9},{11,1... | collective-permute-start | bytes 200 | tf_op jit(solution)/shard_map/ppermute | solution.py:21
  296.9 13.0 %collective-permute-start.13 = (f32[8,8,8]{2,0,1:T(8,128)S(1)}, f32[8,8,8]{2,0,1:T(8,128)S(1)}, u32[]{:S(2)}, u32[]{:S(2)}) collective-permute-start(f32[8,8,8]{2,0,1:T(8,128)S(1)} %get-tuple-element.32), channel_id=1, source_target_pairs={{1,0},{2,1},{3,2},{4,3},{5,4},{6,5},{7,6},{0,7},{9,8},{10,9},{11,1... | collective-permute-start | bytes 6152 | tf_op jit(solution)/shard_map/ppermute | solution.py:21
  302.9 7.2 %collective-permute-start.42 = (f32[1,4,32]{2,0,1:T(1,128)S(1)}, f32[1,4,32]{2,0,1:T(1,128)S(1)}, u32[]{:S(2)}, u32[]{:S(2)}) collective-permute-start(f32[1,4,32]{2,0,1:T(1,128)S(1)} %get-tuple-element.45), channel_id=1, source_target_pairs={{0,64},{64,128},{128,192},{192,256},{256,320},{320,384},{384,448},... | collective-permute-start | bytes 1544 | tf_op jit(solution)/shard_map/ppermute | solution.py:19
  305.2 5.4 %collective-permute-start.43 = (f32[1,4,32]{2,0,1:T(1,128)S(1)}, f32[1,4,32]{2,0,1:T(1,128)S(1)}, u32[]{:S(2)}, u32[]{:S(2)}) collective-permute-start(f32[1,4,32]{2,0,1:T(1,128)S(1)} %get-tuple-element.46), channel_id=1, source_target_pairs={{64,0},{128,64},{192,128},{256,192},{320,256},{384,320},{448,384},... | collective-permute-start | bytes 1544 | tf_op jit(solution)/shard_map/ppermute | solution.py:21
  310.7 15.3 %collective-permute-start.44 = (f32[6,1,32]{2,0,1:T(8,128)S(1)}, f32[6,1,32]{2,0,1:T(8,128)S(1)}, u32[]{:S(2)}, u32[]{:S(2)}) collective-permute-start(f32[6,1,32]{2,0,1:T(8,128)S(1)} %get-tuple-element.41), channel_id=1, source_target_pairs={{0,8},{8,16},{16,24},{24,32},{32,40},{40,48},{48,56},{56,0},{1,9},... | collective-permute-start | bytes 2312 | tf_op jit(solution)/shard_map/ppermute | solution.py:19
  315.4 10.5 %collective-permute-start.45 = (f32[6,1,32]{2,0,1:T(8,128)S(1)}, f32[6,1,32]{2,0,1:T(8,128)S(1)}, u32[]{:S(2)}, u32[]{:S(2)}) collective-permute-start(f32[6,1,32]{2,0,1:T(8,128)S(1)} %get-tuple-element.42), channel_id=1, source_target_pairs={{8,0},{16,8},{24,16},{32,24},{40,32},{48,40},{56,48},{0,56},{9,1},... | collective-permute-start | bytes 2312 | tf_op jit(solution)/shard_map/ppermute | solution.py:21
  320.5 19.3 %collective-permute-start.15 = (f32[8,8,4,64]{3,1,2,0:T(8,128)S(1)}, f32[8,8,4,64]{3,1,2,0:T(8,128)S(1)}, u32[]{:S(2)}, u32[]{:S(2)}) collective-permute-start(f32[8,8,4,64]{3,1,2,0:T(8,128)S(1)} %fusion.28), channel_id=1, source_target_pairs={{8,0},{16,8},{24,16},{32,24},{40,32},{48,40},{56,48},{0,56},{9,1},... | collective-permute-start | bytes 196616 | tf_op jit(solution)/shard_map/ppermute | solution.py:21
  326.1 11.3 %collective-permute-start.46 = (f32[6,6,1]{2,0,1:T(8,128)S(1)}, f32[6,6,1]{2,0,1:T(8,128)S(1)}, u32[]{:S(2)}, u32[]{:S(2)}) collective-permute-start(f32[6,6,1]{2,0,1:T(8,128)S(1)} %get-tuple-element.37), channel_id=1, source_target_pairs={{0,1},{1,2},{2,3},{3,4},{4,5},{5,6},{6,7},{7,0},{8,9},{9,10},{10,1... | collective-permute-start | bytes 440 | tf_op jit(solution)/shard_map/ppermute | solution.py:19
  329.9 9.4 %collective-permute-start.47 = (f32[6,6,1]{2,0,1:T(8,128)S(1)}, f32[6,6,1]{2,0,1:T(8,128)S(1)}, u32[]{:S(2)}, u32[]{:S(2)}) collective-permute-start(f32[6,6,1]{2,0,1:T(8,128)S(1)} %get-tuple-element.38), channel_id=1, source_target_pairs={{1,0},{2,1},{3,2},{4,3},{5,4},{6,5},{7,6},{0,7},{9,8},{10,9},{11,1... | collective-permute-start | bytes 440 | tf_op jit(solution)/shard_map/ppermute | solution.py:21
  341.6 7.2 %collective-permute-start.17 = (f32[8,4,8,64]{3,2,0,1:T(8,128)S(1)}, f32[8,4,8,64]{3,2,0,1:T(8,128)S(1)}, u32[]{:S(2)}, u32[]{:S(2)}) collective-permute-start(f32[8,4,8,64]{3,2,0,1:T(8,128)S(1)} %convolution_bitcast_fusion.1), channel_id=1, source_target_pairs={{64,0},{128,64},{192,128},{256,192},{320,256},{384,320},{448,384},... | collective-permute-start | bytes 196616 | tf_op jit(solution)/shard_map/ppermute | solution.py:21
  346.7 6.9 %collective-permute-start.16 = (f32[8,4,8,64]{3,2,0,1:T(8,128)S(1)}, f32[8,4,8,64]{3,2,0,1:T(8,128)S(1)}, u32[]{:S(2)}, u32[]{:S(2)}) collective-permute-start(f32[8,4,8,64]{3,2,0,1:T(8,128)S(1)} %convolution_bitcast_fusion.1), channel_id=1, source_target_pairs={{0,64},{64,128},{128,192},{192,256},{256,320},{320,384},{384,448},... | collective-permute-start | bytes 196616 | tf_op jit(solution)/shard_map/ppermute | solution.py:19
  354.1 6.5 %collective-permute-start.48 = (f32[1,8,64]{2,0,1:T(1,128)S(1)}, f32[1,8,64]{2,0,1:T(1,128)S(1)}, u32[]{:S(2)}, u32[]{:S(2)}) collective-permute-start(f32[1,8,64]{2,0,1:T(1,128)S(1)} %get-tuple-element.29), channel_id=1, source_target_pairs={{0,64},{64,128},{128,192},{192,256},{256,320},{320,384},{384,448},... | collective-permute-start | bytes 6152 | tf_op jit(solution)/shard_map/ppermute | solution.py:19
  356.1 5.3 %collective-permute-start.49 = (f32[1,8,64]{2,0,1:T(1,128)S(1)}, f32[1,8,64]{2,0,1:T(1,128)S(1)}, u32[]{:S(2)}, u32[]{:S(2)}) collective-permute-start(f32[1,8,64]{2,0,1:T(1,128)S(1)} %get-tuple-element.30), channel_id=1, source_target_pairs={{64,0},{128,64},{192,128},{256,192},{320,256},{384,320},{448,384},... | collective-permute-start | bytes 6152 | tf_op jit(solution)/shard_map/ppermute | solution.py:21
  361.4 11.9 %collective-permute-start.50 = (f32[10,1,64]{2,0,1:T(8,128)S(1)}, f32[10,1,64]{2,0,1:T(8,128)S(1)}, u32[]{:S(2)}, u32[]{:S(2)}) collective-permute-start(f32[10,1,64]{2,0,1:T(8,128)S(1)} %get-tuple-element.23), channel_id=1, source_target_pairs={{0,8},{8,16},{16,24},{24,32},{32,40},{40,48},{48,56},{56,0},{1,9},... | collective-permute-start | bytes 7688 | tf_op jit(solution)/shard_map/ppermute | solution.py:19
  373.5 19.9 %collective-permute-start.52 = (f32[10,10,1]{2,0,1:T(8,128)S(1)}, f32[10,10,1]{2,0,1:T(8,128)S(1)}, u32[]{:S(2)}, u32[]{:S(2)}) collective-permute-start(f32[10,10,1]{2,0,1:T(8,128)S(1)} %get-tuple-element.17), channel_id=1, source_target_pairs={{0,1},{1,2},{2,3},{3,4},{4,5},{5,6},{6,7},{7,0},{8,9},{9,10},{10,1... | collective-permute-start | bytes 1208 | tf_op jit(solution)/shard_map/ppermute | solution.py:19
  375.5 17.9 %collective-permute-start.53 = (f32[10,10,1]{2,0,1:T(8,128)S(1)}, f32[10,10,1]{2,0,1:T(8,128)S(1)}, u32[]{:S(2)}, u32[]{:S(2)}) collective-permute-start(f32[10,10,1]{2,0,1:T(8,128)S(1)} %get-tuple-element.18), channel_id=1, source_target_pairs={{1,0},{2,1},{3,2},{4,3},{5,4},{6,5},{7,6},{0,7},{9,8},{10,9},{11,1... | collective-permute-start | bytes 1208 | tf_op jit(solution)/shard_map/ppermute | solution.py:21
  384.9 8.9 %collective-permute-start.2 = (f32[16,8,4,128]{3,1,2,0:T(8,128)S(1)}, f32[16,8,4,128]{3,1,2,0:T(8,128)S(1)}, u32[]{:S(2)}, u32[]{:S(2)}) collective-permute-start(f32[16,8,4,128]{3,1,2,0:T(8,128)S(1)} %get-tuple-element.7), channel_id=1, source_target_pairs={{0,8},{8,16},{16,24},{24,32},{32,40},{40,48},{48,56},{56,0},{1,9},... | collective-permute-start | bytes 786440 | tf_op jit(solution)/shard_map/ppermute | solution.py:19
  387.3 8.6 %collective-permute-start.3 = (f32[16,8,4,128]{3,1,2,0:T(8,128)S(1)}, f32[16,8,4,128]{3,1,2,0:T(8,128)S(1)}, u32[]{:S(2)}, u32[]{:S(2)}) collective-permute-start(f32[16,8,4,128]{3,1,2,0:T(8,128)S(1)} %get-tuple-element.8), channel_id=1, source_target_pairs={{8,0},{16,8},{24,16},{32,24},{40,32},{48,40},{56,48},{0,56},{9,1},... | collective-permute-start | bytes 786440 | tf_op jit(solution)/shard_map/ppermute | solution.py:21
  396.6 8.9 %collective-permute-start.4 = (f32[8,4,16,128]{3,2,0,1:T(8,128)S(1)}, f32[8,4,16,128]{3,2,0,1:T(8,128)S(1)}, u32[]{:S(2)}, u32[]{:S(2)}) collective-permute-start(f32[8,4,16,128]{3,2,0,1:T(8,128)S(1)} %get-tuple-element.5), channel_id=1, source_target_pairs={{0,64},{64,128},{128,192},{192,256},{256,320},{320,384},{384,448},... | collective-permute-start | bytes 786440 | tf_op jit(solution)/shard_map/ppermute | solution.py:19
  398.5 8.4 %collective-permute-start.5 = (f32[8,4,16,128]{3,2,0,1:T(8,128)S(1)}, f32[8,4,16,128]{3,2,0,1:T(8,128)S(1)}, u32[]{:S(2)}, u32[]{:S(2)}) collective-permute-start(f32[8,4,16,128]{3,2,0,1:T(8,128)S(1)} %get-tuple-element.6), channel_id=1, source_target_pairs={{64,0},{128,64},{192,128},{256,192},{320,256},{384,320},{448,384},... | collective-permute-start | bytes 786440 | tf_op jit(solution)/shard_map/ppermute | solution.py:21
  (10 other events, 704.8 us)
where the time goes:
time: 416 us; the launch traced here: 409 us
  starting transfers between devices  240 us (58%)
  blocking collectives  104 us (25%)
  waiting for transfers between devices  46.1 us (11%)
  matrix products  11.2 us (3%)
  local copies, waits for them, and re-layouts  4.52 us (1%)
    ppermute x27, starting transfers between devices, with_halo(): lax.ppermute(head, axis, [((i + 1) % count, i) for i in range(count)])  141 us
    unnamed x1, blocking collectives  104 us
    ppermute x27, starting transfers between devices, with_halo(): lax.ppermute(tail, axis, [(i, (i + 1) % count) for i in range(count)])  98.4 us
    ppermute x27, waiting for transfers between devices, with_halo(): lax.ppermute(head, axis, [((i + 1) % count, i) for i in range(count)])  31.4 us
    ppermute x27, waiting for transfers between devices, with_halo(): lax.ppermute(tail, axis, [(i, (i + 1) % count) for i in range(count)])  14.7 us
  transfers between devices with their start and end apart: 54, of which 21 were waited for; matrix products, arithmetic and copies ran while one was open for 4% of the time, Pallas kernels for 0%

commit v1 on v0

v1 whole, which is shorter than its diff:
```python
import functools

import jax
import jax.numpy as jnp
import numpy as np
from jax import lax
from jax.experimental import pallas as pl
from jax.experimental.pallas import tpu as pltpu
from jax.sharding import PartitionSpec as P

MESH = pl.DeviceIdType.MESH
TERMS = 4
REACH = 8
F32 = jnp.float32
BF16 = jnp.bfloat16
NEAR = [(dx, dy) for dx in (-1, 0, 1) for dy in (-1, 0, 1) if (dx, dy) != (0, 0)]
AXES = ("gx", "gy", "gz")


def spline_np(off):
    off = np.asarray(off)
    return np.where((off == 1) | (off == 2), 0.75, np.where((off == 0) | (off == 3), 0.25, 0.0))


def composite_np(levels):
    box = np.ones(2**levels)
    return np.convolve(np.convolve(box, box), box) / 4.0**levels


def composite_at(levels, fine, cell):
    taps = composite_np(levels)
    off = fine - (cell * 2**levels - (2**levels - 1))
    return np.where((off >= 0) & (off < len(taps)), taps[np.clip(off, 0, len(taps) - 1)], 0.0)


def tables():
    x = np.arange(16)[:, None]
    i = np.arange(10)[None, :]
    px = spline_np(x - 2 * i + 3)
    j = np.arange(16)[None, :]
    py = np.where(j < 10, spline_np(x - 2 * j + 3), 0.0)
    pp = np.einsum("xi,yj->xyij", px, py).reshape(256, 160)
    row = np.arange(128)[:, None]
    lane = np.arange(128)[None, :]
    rt = spline_np(lane - 2 * row + 3)
    m = np.arange(24)[:, None]
    yi = np.arange(32)[None, :]
    ry = np.where(m < 10, spline_np(yi - 2 * m - 5), np.where(m >= 16, spline_np(yi - 2 * m + 23), 0.0))
    ry2 = np.concatenate([ry, ry], axis=1)
    r = np.arange(16)
    a, b = r >> 2, r & 3
    wa = composite_at(4, np.arange(16)[None, :], a[:, None] - 1) * (a < 3)[:, None]
    wb = composite_at(4, np.arange(16)[None, :], b[:, None] - 1) * (b < 3)[:, None]
    w9 = np.einsum("rx,ry->rxy", wa, wb).reshape(16, 256)
    ci = np.arange(10)[:, None] - 1
    cj = np.arange(16)[:, None] - 1
    pa = composite_at(3, ci, a[None, :] - 1) * (a < 3)[None, :]
    pb = composite_at(3, cj, b[None, :] - 1) * (b < 3)[None, :] * (np.arange(16) < 10)[:, None]
    p3 = np.einsum("ir,jr->ijr", pa, pb).reshape(160, 16)
    mm = np.arange(32)[:, None]
    zf = np.arange(128)[None, :]
    cell = np.where(mm < 16, 55 + mm, mm - 17)
    edge = np.where((mm % 16) < 10, spline_np(zf - 2 * cell + 1), 0.0)
    t = np.arange(16)[:, None]
    sel = (zf == np.where(t < 8, 120 + t, t - 8)).astype(np.float64)
    bf = lambda v: np.asarray(v, np.float32).astype(jnp.bfloat16)
    fl = lambda v: np.asarray(v, np.float32)
    return [bf(pp), bf(rt), bf(rt.T), bf(ry2), fl(w9), fl(p3), bf(edge), bf(sel)]


def split(v):
    hi = v.astype(BF16)
    return hi, (v - hi.astype(F32)).astype(BF16)


def dot(a, b, dims=((1,), (0,))):
    return lax.dot_general(a, b, (dims, ((), ())), preferred_element_type=F32)


def dot3(a, b, dims=((1,), (0,))):
    ah, al = split(a)
    bh, bl = split(b)
    return dot(ah, bh, dims) + dot(ah, bl, dims) + dot(al, bh, dims)


def iota(shape, dim):
    return lax.broadcasted_iota(jnp.int32, shape, dim)


def by_term(values, index):
    out = jnp.where(index == 0, values[0], values[1])
    for t in range(2, TERMS):
        out = jnp.where(index == t, values[t], out)
    return out


def composite4(fine, cell):
    off = fine - (cell * 16 - 15)

    def pairs(shift):
        m = jnp.maximum(off + shift, 0).astype(F32)
        return m * (m - 1.0) * 0.5

    return (pairs(2) - 3.0 * pairs(-14) + 3.0 * pairs(-30) - pairs(-46)) * (1.0 / 256.0)


def kernel(
    sizes,
    charges, exps, amps, top_x, top_y, top_z,
    c_pp, c_rt, c_r, c_ry, c_w9, c_p3, c_edge, c_sel,
    out,
    ext, v0, y0, fext, q2, v1, y1,
    rx1, rx2, rx3, tx1, tx2, tx3,
    zs0, zs1, zr0, zr1,
    taps, inv,
    a_send, a_recv, b_send, b_recv, t_send, t_recv, z_send, z_recv,
):
    nx, ny, nz = sizes
    me = [lax.axis_index(axis) for axis in AXES]
    gx, gy, gz = me

    def at(dx, dy, dz):
        return (lax.rem(gx + dx + nx, nx), lax.rem(gy + dy + ny, ny), lax.rem(gz + dz + nz, nz))

    partners = [(dx, dy, 0) for dx, dy in NEAR]
    partners += [(o, 0, 0) for o in range(2, nx - 1)]
    partners += [(0, o, 0) for o in range(2, ny - 1)]
    partners += [(0, 0, o) for o in range(1, nz)]
    barrier = pltpu.get_barrier_semaphore()
    for p in partners:
        pl.semaphore_signal(barrier, inc=1, device_id=at(*p), device_id_type=MESH)

    ext[8:24, 8:24, :] = charges[...]
    flat = charges[...].reshape(256, 128)
    part = dot3(c_w9[...], flat)
    zi = iota((128, 128), 0)
    lane = iota((128, 128), 1)
    slot = lane & 15
    place = jnp.where(((lane >> 4) == gz) & (slot < 10), composite4(zi, slot - 1), 0.0)
    tx1[...] = dot3(part, place)
    rx1[0] = tx1[...]
    pl.semaphore_wait(barrier, len(partners))

    def remote(src, dst, send, recv, where):
        return pltpu.make_async_remote_copy(
            src_ref=src, dst_ref=dst, send_sem=send, recv_sem=recv, device_id=at(*where), device_id_type=MESH
        )

    def top_copies(step, src, dst):
        shift = [(1, 0, 0), (0, 1, 0), (0, 0, 1)][step]
        return [
            remote(
                src, dst.at[o], t_send.at[step * 8 + o], t_recv.at[step * 8 + o],
                (shift[0] * o, shift[1] * o, shift[2] * o),
            )
            for o in range(1, sizes[step])
        ]

    source_a = {-1: pl.ds(8, 8), 0: pl.ds(8, 16), 1: pl.ds(16, 8)}
    target_a = {-1: pl.ds(24, 8), 0: pl.ds(8, 16), 1: pl.ds(0, 8)}
    copies_t1 = top_copies(0, tx1, rx1)
    copies_a = [
        remote(
            ext.at[source_a[dx], source_a[dy], :], ext.at[target_a[dx], target_a[dy], :],
            a_send.at[n], a_recv.at[n], (dx, dy, 0),
        )
        for n, (dx, dy) in enumerate(NEAR)
    ]
    for copy in copies_t1:
        copy.start()
    for copy in copies_a:
        copy.start()

    for level in range(2):
        for r in range(TERMS):
            e = jnp.full((8, 128), exps[level, r], F32)
            weights = [jnp.exp(-e * float(k * k)) for k in range(REACH + 1)]
            total = weights[1]
            for k in range(2, REACH + 1):
                total = total + weights[k]
            inverse = 1.0 / (1.0 + 2.0 * total)
            inv[level * TERMS + r] = inverse
            for k in range(REACH + 1):
                taps[(level * TERMS + r) * 9 + k] = weights[k] * inverse * amps[level, r]

    def band(level, term, offset):
        if isinstance(term, int):
            e = exps[level, term]
            scale = inv[level * TERMS + term][0:1, 0:1]
        else:
            e = by_term([exps[level, t] for t in range(TERMS)], term)
            scale = by_term([inv[level * TERMS + t][0:1, 0:1] for t in range(TERMS)], term)
        far = offset.astype(F32)
        return jnp.where(jnp.abs(offset) <= REACH, jnp.exp(-e * (far * far)) * scale, 0.0)

    def tripled(matrix, copy_at):
        hi = matrix.astype(BF16)
        lo = (matrix - hi.astype(F32)).astype(BF16)
        return jnp.where(copy_at == 1, lo.astype(F32), hi.astype(F32)).astype(BF16)

    row = iota((64, 96), 0)
    col = iota((64, 96), 1)
    col32 = col & 31
    band_y0 = tripled(band(0, row >> 4, col32 - 8 - (row & 15)), col >> 5)
    where1 = jnp.where(col32 < 18, col32 - 9, jnp.where(col32 >= 24, col32 - 15, 1000))
    off1 = jnp.where((row & 15) < 10, where1 - ((row & 15) - 1), 1000)
    band_y1 = tripled(band(1, row >> 4, off1), col >> 5)

    def tops(table, own, shape_sizes, first):
        r8 = iota((16, 8), 0)
        p8 = iota((16, 8), 1)
        c8 = iota((8, 128), 0)
        l8 = iota((8, 128), 1)
        rr = iota((16, 128), 0)
        ll = iota((16, 128), 1)
        if first:
            mine, theirs = r8 >> 2, (l8 & 15) >> 2
            same = (rr & 3) == (ll & 3)
        else:
            mine, theirs = r8 & 3, l8 & 3
            same = (rr >> 2) == ((ll & 15) >> 2)
        pick_rows = (p8 == ((own + mine + 7) & 7)).astype(F32)
        pick_cols = (c8 == ((own - (l8 >> 4) + theirs + 15) & 7)).astype(F32)
        whole = dot3(dot3(pick_rows, table), pick_cols)
        valid = ((rr >> 2) < 3) & ((rr & 3) < 3) & (((ll & 15) >> 2) < 3) & ((ll & 3) < 3)
        return jnp.where(same & valid, whole, 0.0)

    mix_x = tops(top_x[...], gx, sizes, True)
    for n, copy in enumerate(copies_t1):
        copy.wait_recv()
    tx2[...] = dot3(mix_x, rx1[...].reshape(128, 128))
    rx2[0] = tx2[...]
    copies_t2 = top_copies(1, tx2, rx2)
    for copy in copies_t2:
        copy.start()

    for copy in copies_a:
        copy.wait_recv()

    for i in range(10):
        rx = 0.25 * (ext[2 * i + 5] + ext[2 * i + 8]) + 0.75 * (ext[2 * i + 6] + ext[2 * i + 7])
        hi, lo = split(rx)
        cells = dot(c_ry[...], jnp.concatenate([hi, lo], axis=0))
        fext[8 + i, 8:24, :] = cells[0:16]
        q2[i] = cells[16:24]

    xs = {-1: pl.ds(10, 8), 0: pl.ds(8, 10), 1: pl.ds(8, 8)}
    xd = {-1: pl.ds(18, 8), 0: pl.ds(8, 10), 1: pl.ds(0, 8)}
    yd = {-1: pl.ds(24, 8), 0: pl.ds(8, 16), 1: pl.ds(0, 8)}
    copies_b = []
    for n, (dx, dy) in enumerate(NEAR):
        if dy == -1:
            src = q2.at[pl.ds(xs[dx].start - 8, xs[dx].size)]
        else:
            src = fext.at[xs[dx], pl.ds(8, 16 if dy == 0 else 8), :]
        copies_b.append(
            remote(src, fext.at[xd[dx], yd[dy], :], b_send.at[n], b_recv.at[n], (dx, dy, 0))
        )
    for copy in copies_b:
        copy.start()

    mix_y = tops(top_y[...], gy, sizes, False)
    for copy in copies_t2:
        copy.wait_recv()
    tx3[...] = dot3(mix_y, rx2[...].reshape(128, 128))
    rx3[0] = tx3[...]
    copies_t3 = top_copies(2, tx3, rx3)
    for copy in copies_t3:
        copy.start()

    def smooth_y(source, band_y, target, at_x):
        hi, lo = split(source[at_x])
        target[at_x] = dot(band_y, jnp.concatenate([hi, hi, lo], axis=0))

    def level0_y(step, carry):
        for u in range(8):
            smooth_y(ext, band_y0, v0, step * 8 + u)
        return carry

    lax.fori_loop(0, 4, level0_y, 0)

    def smooth_x(source, target, level, count, stride):
        for r in range(TERMS):
            w = [taps[(level * TERMS + r) * 9 + k] for k in range(9)]
            for half in range(2):
                rows = slice(r * 16 + half * 8, r * 16 + half * 8 + 8)
                for x in range(count):
                    acc = w[0] * source[x + 8, rows, :]
                    for k in range(1, 9):
                        acc = acc + w[k] * (source[x + 8 - k, rows, :] + source[x + 8 + k, rows, :])
                    target[x * 16 + half * 8 : x * 16 + half * 8 + 8, r * 128 : r * 128 + 128] = acc

    smooth_x(v0, y0, 0, 16, 16)

    zi = iota((128, 128), 0)
    zo = iota((128, 128), 1)
    band_z0 = jnp.concatenate([band(0, r, zi - zo) for r in range(TERMS)], axis=0)
    h_row = iota((16, 128), 0)
    h_lane = iota((16, 128), 1)
    h_out = jnp.where(h_row < 8, h_row - 8, h_row + 120)
    edge_z0 = jnp.concatenate([band(0, r, h_lane - h_out) for r in range(TERMS)], axis=1)
    y0h, y0l = split(y0[...])
    eh, el = split(edge_z0)
    nt = ((1,), (1,))
    zs0[...] = dot(eh, y0h, nt) + dot(eh, y0l, nt) + dot(el, y0h, nt)
    left, right = (0, 0, -1), (0, 0, 1)
    copies_z0 = [
        remote(zs0.at[pl.ds(0, 8)], zr0.at[pl.ds(0, 8)], z_send.at[0], z_recv.at[0], left),
        remote(zs0.at[pl.ds(8, 8)], zr0.at[pl.ds(8, 8)], z_send.at[1], z_recv.at[1], right),
    ]
    for copy in copies_z0:
        copy.start()
    bh, bl = split(band_z0)
    out[...] = (dot(y0h, bh) + dot(y0h, bl) + dot(y0l, bh)).reshape(16, 16, 128)

    g_row = iota((32, 128), 0)
    g_cell = iota((32, 128), 1) - 1
    g_out = jnp.where(g_row < 16, g_row - 9, g_row + 47)
    g_out = jnp.where((g_row & 15) < 10, g_out, 1000)
    mains, edges = [], []
    for r in range(TERMS):
        gh, gl = split(band(1, r, zi - zo))
        ch, cl = split(dot(c_r[...], gh) + dot(c_r[...], gl))
        mains.append(dot(ch, c_rt[...]) + dot(cl, c_rt[...]))
        eh, el = split(band(1, r, g_cell - g_out))
        edges.append(dot(eh, c_rt[...]) + dot(el, c_rt[...]))
    main_h, main_l = split(jnp.concatenate(mains, axis=0))
    edge_h, edge_l = split(jnp.concatenate(edges, axis=1))

    p_at = iota((128, 64), 1)
    z_at = iota((128, 64), 0)
    cell = ((p_at - 8 * gz + 65) & 63) - 1
    spread = jnp.where(cell <= 8, composite4(z_at, cell), 0.0)
    q_at = iota((64, 128), 0)
    k_at = iota((64, 128), 1)
    picked = jnp.where((q_at == ((8 * (k_at >> 4) + (k_at & 15) + 63) & 63)) & ((k_at & 15) < 10), 1.0, 0.0)
    top_mix = dot3(dot3(spread, top_z[...]), picked)

    for copy in copies_b:
        copy.wait_recv()

    def level1_y(step, carry):
        for u in range(13):
            smooth_y(fext, band_y1, v1, step * 13 + u)
        return carry

    lax.fori_loop(0, 2, level1_y, 0)
    smooth_x(v1, y1, 1, 10, 16)
    y1h, y1l = split(y1[...])
    zs1[:, 0:160] = dot(edge_h, y1h, nt) + dot(edge_h, y1l, nt) + dot(edge_l, y1h, nt)
    zs1[:, 160:256] = jnp.zeros((32, 96), F32)
    copies_z1 = [
        remote(zs1.at[pl.ds(0, 16)], zr1.at[pl.ds(0, 16)], z_send.at[2], z_recv.at[2], left),
        remote(zs1.at[pl.ds(16, 16)], zr1.at[pl.ds(16, 16)], z_send.at[3], z_recv.at[3], right),
    ]
    for copy in copies_z1:
        copy.start()
    level1 = dot(y1h, main_h) + dot(y1h, main_l) + dot(y1l, main_h)

    for copy in copies_t3:
        copy.wait_recv()
    total = rx3[0]
    for o in range(1, nz):
        total = total + rx3[o]
    level1 = level1 + dot3(c_p3[...], dot3(total, top_mix, nt))

    for copy in copies_z0:
        copy.wait_recv()
    tn = ((0,), (0,))
    zh, zl = split(zr0[...])
    potential = out[...].reshape(256, 128) + dot(zh, c_sel[...], tn) + dot(zl, c_sel[...], tn)
    for copy in copies_z1:
        copy.wait_recv()
    zh, zl = split(zr1[...])
    side = dot(zh, c_edge[...], tn) + dot(zl, c_edge[...], tn)
    level1 = level1 + side[0:160]
    lh, ll = split(level1)
    out[...] = (potential + dot(c_pp[...], lh) + dot(c_pp[...], ll)).reshape(16, 16, 128)

    for copy in copies_t1 + copies_a + copies_t2 + copies_b + copies_t3 + copies_z0 + copies_z1:
        copy.wait_send()


def solution(mesh):
    sizes = tuple(mesh.shape[axis] for axis in AXES)
    consts = tables()

    def local(charges, exponents, amplitudes, top_x, top_y, top_z):
        vmem = pl.BlockSpec(memory_space=pltpu.VMEM)
        smem = pl.BlockSpec(memory_space=pltpu.SMEM)
        return pl.pallas_call(
            functools.partial(kernel, sizes),
            out_shape=jax.ShapeDtypeStruct(charges.shape, F32),
            in_specs=[vmem, smem, smem, vmem, vmem, vmem] + [vmem] * len(consts),
            out_specs=vmem,
            scratch_shapes=[
                pltpu.VMEM((32, 32, 128), F32),
                pltpu.VMEM((32, 64, 128), F32),
                pltpu.VMEM((256, 512), F32),
                pltpu.VMEM((26, 32, 128), F32),
                pltpu.VMEM((10, 8, 128), F32),
                pltpu.VMEM((26, 64, 128), F32),
                pltpu.VMEM((160, 512), F32),
                pltpu.VMEM((8, 16, 128), F32),
                pltpu.VMEM((8, 16, 128), F32),
                pltpu.VMEM((8, 16, 128), F32),
                pltpu.VMEM((16, 128), F32),
                pltpu.VMEM((16, 128), F32),
                pltpu.VMEM((16, 128), F32),
                pltpu.VMEM((16, 256), F32),
                pltpu.VMEM((32, 256), F32),
                pltpu.VMEM((16, 256), F32),
                pltpu.VMEM((32, 256), F32),
                pltpu.VMEM((72, 8, 128), F32),
                pltpu.VMEM((8, 8, 128), F32),
                pltpu.SemaphoreType.DMA((8,)),
                pltpu.SemaphoreType.DMA((8,)),
                pltpu.SemaphoreType.DMA((8,)),
                pltpu.SemaphoreType.DMA((8,)),
                pltpu.SemaphoreType.DMA((24,)),
                pltpu.SemaphoreType.DMA((24,)),
                pltpu.SemaphoreType.DMA((4,)),
                pltpu.SemaphoreType.DMA((4,)),
            ],
            compiler_params=pltpu.CompilerParams(
                collective_id=0, has_side_effects=True, vmem_limit_bytes=40 * 2**20
            ),
        )(charges, exponents, amplitudes, top_x, top_y, top_z, *[jnp.asarray(c) for c in consts])

    in_specs = (P("gx", "gy", "gz"), P(), P(), P(), P(), P())
    return jax.shard_map(local, mesh=mesh, in_specs=in_specs, out_specs=P("gx", "gy", "gz"), check_vma=False)
```

time: 416 us -> 47.1 us (0.11); the launches traced: 409 us -> 46.5 us
  starting transfers between devices: 240 us -> 0 us
  blocking collectives: 104 us -> 0 us
  waiting for transfers between devices: 46.1 us -> 0 us
  Pallas kernels: 0 us -> 36 us
  matrix products: 11.2 us -> 0 us
  local copies, waits for them, and re-layouts: 4.52 us -> 10.5 us
    ppermute x54 -> x0, starting transfers between devices: 240 us -> none  [the longest x27 141 us: with_halo(): lax.ppermute(head, axis, [((i + 1) % count, i) for i in range(count)])]
    unnamed x1 -> x0, blocking collectives: 104 us -> none
    ppermute x54 -> x0, waiting for transfers between devices: 46.1 us -> none  [the longest x27 31.4 us: with_halo(): lax.ppermute(head, axis, [((i + 1) % count, i) for i in range(count)])]
    pallas_call x0 -> x1, Pallas kernels: none -> 36 us  [local(): pl.pallas_call(functools.partial(kernel, sizes), out_shape=jax.ShapeDtype...]
    dot_general x37 -> x0, matrix products: 11.2 us -> none  [the longest x8 2.53 us: apply_three(): field = jnp.einsum('xyz,zc->xyc', field, band_z, precision=HIGHEST)]
    unnamed x12 -> x29, local copies, waits for them, and re-layouts: 0.28 us -> 10.5 us
  transfers between devices with their start and end apart: 54 -> 0, of which waited for: 21 -> 0; matrix products, arithmetic and copies ran while one was open for 4% -> 0% of each run, Pallas kernels for 0% -> 0%
where the time goes in v1:
time: 47.1 us; the launch traced here: 46.5 us
  Pallas kernels  36 us (76%)
  local copies, waits for them, and re-layouts  10.5 us (22%)
    pallas_call x1, Pallas kernels, local(): pl.pallas_call(functools.partial(kernel, sizes), out_shape=jax.ShapeDtype...  36 us
    unnamed x29, local copies, waits for them, and re-layouts  10.5 us

profile of v1, /device:TPU:1, one launch (start us, length us, event | category | flops | bytes accessed | tf_op | source)
XLA Modules:
  0.0 46.5 jit_solution(3920334592641341862)
XLA Ops:
  0.0 0.0 copy-start.11
  0.0 0.0 copy-start.7
  0.0 0.7 %copy-done.11 = bf16[16,128]{1,0:T(8,128)(2,1)S(1)} copy-done((bf16[16,128]{1,0:T(8,128)(2,1)S(1)}, bf16[16,128]{1,0:T(8,128)(2,1)}, u32[]{:S(2)}) %copy-start.11) | copy-done | bytes 4120
  0.7 0.0 copy-done.7
  0.7 0.0 copy-start
  0.7 0.9 %copy-done = f32[16,16,128]{2,1,0:T(8,128)S(1)} copy-done((f32[16,16,128]{2,1,0:T(8,128)S(1)}, f32[16,16,128]{2,1,0:T(8,128)}, u32[]{:S(2)}) %copy-start) | copy-done | bytes 131096
  1.6 0.0 copy-start.1
  1.6 0.9 %copy-done.1 = bf16[256,160]{1,0:T(8,128)(2,1)S(1)} copy-done((bf16[256,160]{1,0:T(8,128)(2,1)S(1)}, bf16[256,160]{1,0:T(8,128)(2,1)}, u32[]{:S(2)}) %copy-start.1) | copy-done | bytes 81944
  2.5 0.0 copy-start.2
  2.5 0.9 %copy-done.2 = f32[160,16]{1,0:T(8,128)S(1)} copy-done((f32[160,16]{1,0:T(8,128)S(1)}, f32[160,16]{1,0:T(8,128)}, u32[]{:S(2)}) %copy-start.2) | copy-done | bytes 10264
  3.4 0.0 copy-start.3
  3.4 0.8 %copy-done.3 = f32[64,64]{1,0:T(8,128)S(1)} copy-done((f32[64,64]{1,0:T(8,128)S(1)}, f32[64,64]{1,0:T(8,128)}, u32[]{:S(2)}) %copy-start.3) | copy-done | bytes 16408
  4.2 0.0 copy-start.4
  4.2 0.8 %copy-done.4 = bf16[128,128]{1,0:T(8,128)(2,1)S(1)} copy-done((bf16[128,128]{1,0:T(8,128)(2,1)S(1)}, bf16[128,128]{1,0:T(8,128)(2,1)}, u32[]{:S(2)}) %copy-start.4) | copy-done | bytes 32792
  4.9 0.0 copy-start.5
  4.9 0.8 %copy-done.5 = bf16[128,128]{1,0:T(8,128)(2,1)S(1)} copy-done((bf16[128,128]{1,0:T(8,128)(2,1)S(1)}, bf16[128,128]{1,0:T(8,128)(2,1)}, u32[]{:S(2)}) %copy-start.5) | copy-done | bytes 32792
  5.7 0.0 copy-start.6
  5.7 0.7 %copy-done.6 = f32[16,256]{1,0:T(8,128)S(1)} copy-done((f32[16,256]{1,0:T(8,128)S(1)}, f32[16,256]{1,0:T(8,128)}, u32[]{:S(2)}) %copy-start.6) | copy-done | bytes 16408
  6.4 0.0 copy-start.8
  6.4 0.7 %copy-done.8 = bf16[24,64]{1,0:T(8,128)(2,1)S(1)} copy-done((bf16[24,64]{1,0:T(8,128)(2,1)S(1)}, bf16[24,64]{1,0:T(8,128)(2,1)}, u32[]{:S(2)}) %copy-start.8) | copy-done | bytes 3096
  7.1 0.0 copy-start.9
  7.1 0.7 %copy-done.9 = f32[8,8]{1,0:T(8,128)S(1)} copy-done((f32[8,8]{1,0:T(8,128)S(1)}, f32[8,8]{1,0:T(8,128)}, u32[]{:S(2)}) %copy-start.9) | copy-done | bytes 280
  7.8 0.0 copy-start.10
  7.8 0.7 %copy-done.10 = f32[8,8]{1,0:T(8,128)S(1)} copy-done((f32[8,8]{1,0:T(8,128)S(1)}, f32[8,8]{1,0:T(8,128)}, u32[]{:S(2)}) %copy-start.10) | copy-done | bytes 280
  8.5 0.0 copy-start.12
  8.5 0.7 %copy-done.12 = f32[2,4]{1,0:T(2,128)S(1)} copy-done((f32[2,4]{1,0:T(2,128)S(1)}, f32[2,4]{1,0:T(2,128)}, u32[]{:S(2)}) %copy-start.12) | copy-done | bytes 56
  9.2 0.0 copy-start.13
  9.2 0.7 %copy-done.13 = f32[2,4]{1,0:T(2,128)S(1)} copy-done((f32[2,4]{1,0:T(2,128)S(1)}, f32[2,4]{1,0:T(2,128)}, u32[]{:S(2)}) %copy-start.13) | copy-done | bytes 56
  9.8 36.0 %shard_map.136 = f32[16,16,128]{2,1,0:T(8,128)S(1)} custom-call(f32[16,16,128]{2,1,0:T(8,128)S(1)} %copy-done, f32[2,4]{1,0:T(2,128)S(1)} %copy-done.12, f32[2,4]{1,0:T(2,128)S(1)} %copy-done.13, f32[8,8]{1,0:T(8,128)S(1)} %copy-done.9, f32[8,8]{1,0:T(8,128)S(1)} %copy-done.10, f32[64,64]{1,0:T(8,128)S(1)} %copy-done.3, bf16[256,160]{1,0:T(8,128)(2,1)S(1)} %copy-done.1, ...), custom_call_target="tpu_custom_call" | custom-call | tf_op jit(solution)/shard_map/pallas_call | solution.py:391
  45.8 0.7 %copy.16 = f32[16,16,128]{2,1,0:T(8,128)} copy(f32[16,16,128]{2,1,0:T(8,128)S(1)} %shard_map.136) | data formatting | bytes 262144
Async XLA Ops:
  0.0 0.7 %copy-start.11 = (bf16[16,128]{1,0:T(8,128)(2,1)S(1)}, bf16[16,128]{1,0:T(8,128)(2,1)}, u32[]{:S(2)}) copy-start(bf16[16,128]{1,0:T(8,128)(2,1)} %constant.23.clone.c_sel) | copy-start | bytes 12292
  0.0 0.7 %copy-start.7 = (bf16[32,128]{1,0:T(8,128)(2,1)S(1)}, bf16[32,128]{1,0:T(8,128)(2,1)}, u32[]{:S(2)}) copy-start(bf16[32,128]{1,0:T(8,128)(2,1)} %constant.22.clone.c_edge) | copy-start | bytes 24580
  0.7 0.9 %copy-start = (f32[16,16,128]{2,1,0:T(8,128)S(1)}, f32[16,16,128]{2,1,0:T(8,128)}, u32[]{:S(2)}) copy-start(f32[16,16,128]{2,1,0:T(8,128)} %charges.1) | copy-start | bytes 393220
  1.6 0.9 %copy-start.1 = (bf16[256,160]{1,0:T(8,128)(2,1)S(1)}, bf16[256,160]{1,0:T(8,128)(2,1)}, u32[]{:S(2)}) copy-start(bf16[256,160]{1,0:T(8,128)(2,1)} %constant.16.clone.c_pp) | copy-start | bytes 245764
  2.5 0.9 %copy-start.2 = (f32[160,16]{1,0:T(8,128)S(1)}, f32[160,16]{1,0:T(8,128)}, u32[]{:S(2)}) copy-start(f32[160,16]{1,0:T(8,128)} %constant.21.clone.c_p3) | copy-start | bytes 30724
  3.4 0.8 %copy-start.3 = (f32[64,64]{1,0:T(8,128)S(1)}, f32[64,64]{1,0:T(8,128)}, u32[]{:S(2)}) copy-start(f32[64,64]{1,0:T(8,128)} %top_z.1) | copy-start | bytes 49156
  4.2 0.8 %copy-start.4 = (bf16[128,128]{1,0:T(8,128)(2,1)S(1)}, bf16[128,128]{1,0:T(8,128)(2,1)}, u32[]{:S(2)}) copy-start(bf16[128,128]{1,0:T(8,128)(2,1)} %constant.18.clone.c_r) | copy-start | bytes 98308
  4.9 0.8 %copy-start.5 = (bf16[128,128]{1,0:T(8,128)(2,1)S(1)}, bf16[128,128]{1,0:T(8,128)(2,1)}, u32[]{:S(2)}) copy-start(bf16[128,128]{1,0:T(8,128)(2,1)} %constant.17.clone.c_rt) | copy-start | bytes 98308
  5.7 0.7 %copy-start.6 = (f32[16,256]{1,0:T(8,128)S(1)}, f32[16,256]{1,0:T(8,128)}, u32[]{:S(2)}) copy-start(f32[16,256]{1,0:T(8,128)} %constant.20.clone.c_w9) | copy-start | bytes 49156
  6.4 0.7 %copy-start.8 = (bf16[24,64]{1,0:T(8,128)(2,1)S(1)}, bf16[24,64]{1,0:T(8,128)(2,1)}, u32[]{:S(2)}) copy-start(bf16[24,64]{1,0:T(8,128)(2,1)} %constant.19.clone.c_ry) | copy-start | bytes 9220
  7.1 0.7 %copy-start.9 = (f32[8,8]{1,0:T(8,128)S(1)}, f32[8,8]{1,0:T(8,128)}, u32[]{:S(2)}) copy-start(f32[8,8]{1,0:T(8,128)} %top_x.1) | copy-start | bytes 772
  7.8 0.7 %copy-start.10 = (f32[8,8]{1,0:T(8,128)S(1)}, f32[8,8]{1,0:T(8,128)}, u32[]{:S(2)}) copy-start(f32[8,8]{1,0:T(8,128)} %top_y.1) | copy-start | bytes 772
  8.5 0.7 %copy-start.12 = (f32[2,4]{1,0:T(2,128)S(1)}, f32[2,4]{1,0:T(2,128)}, u32[]{:S(2)}) copy-start(f32[2,4]{1,0:T(2,128)} %exps.1) | copy-start | bytes 100
  9.2 0.7 %copy-start.13 = (f32[2,4]{1,0:T(2,128)S(1)}, f32[2,4]{1,0:T(2,128)}, u32[]{:S(2)}) copy-start(f32[2,4]{1,0:T(2,128)} %amps.1) | copy-start | bytes 100

commit v2 on v1

--- a/solution.py
+++ b/solution.py
@@ -52,11 +52,7 @@
     wa = composite_at(4, np.arange(16)[None, :], a[:, None] - 1) * (a < 3)[:, None]
     wb = composite_at(4, np.arange(16)[None, :], b[:, None] - 1) * (b < 3)[:, None]
     w9 = np.einsum("rx,ry->rxy", wa, wb).reshape(16, 256)
-    ci = np.arange(10)[:, None] - 1
-    cj = np.arange(16)[:, None] - 1
-    pa = composite_at(3, ci, a[None, :] - 1) * (a < 3)[None, :]
-    pb = composite_at(3, cj, b[None, :] - 1) * (b < 3)[None, :] * (np.arange(16) < 10)[:, None]
-    p3 = np.einsum("ir,jr->ijr", pa, pb).reshape(160, 16)
+    p4 = w9.T
     mm = np.arange(32)[:, None]
     zf = np.arange(128)[None, :]
     cell = np.where(mm < 16, 55 + mm, mm - 17)
@@ -64,8 +60,19 @@
     t = np.arange(16)[:, None]
     sel = (zf == np.where(t < 8, 120 + t, t - 8)).astype(np.float64)
     bf = lambda v: np.asarray(v, np.float32).astype(jnp.bfloat16)
-    fl = lambda v: np.asarray(v, np.float32)
-    return [bf(pp), bf(rt), bf(rt.T), bf(ry2), fl(w9), fl(p3), bf(edge), bf(sel)]
+    lo = lambda v: np.asarray(v, np.float32) - bf(v).astype(np.float32)
+    packed = np.zeros((464, 256), jnp.bfloat16)
+    packed[0:256, 0:160] = bf(pp)
+    packed[0:256, 160:176] = bf(p4)
+    packed[0:256, 176:192] = bf(lo(p4))
+    packed[256:384, 0:128] = bf(rt)
+    packed[256:384, 128:256] = bf(rt.T)
+    packed[384:416, 0:128] = bf(edge)
+    packed[384:408, 128:192] = bf(ry2)
+    packed[416:432, 0:128] = bf(sel)
+    packed[432:448] = bf(w9)
+    packed[448:464] = bf(lo(w9))
+    return packed
 
 
 def split(v):
@@ -106,9 +113,9 @@
 
 def kernel(
     sizes,
-    charges, exps, amps, top_x, top_y, top_z,
-    c_pp, c_rt, c_r, c_ry, c_w9, c_p3, c_edge, c_sel,
+    charges, exps_in, amps_in, top_x_in, top_y_in, top_z_in, table_in,
     out,
+    exps, amps, top_x, top_y, top_z, table, load_sem,
     ext, v0, y0, fext, q2, v1, y1,
     rx1, rx2, rx3, tx1, tx2, tx3,
     zs0, zs1, zr0, zr1,
@@ -130,15 +137,22 @@
     for p in partners:
         pl.semaphore_signal(barrier, inc=1, device_id=at(*p), device_id_type=MESH)
 
-    ext[8:24, 8:24, :] = charges[...]
-    flat = charges[...].reshape(256, 128)
-    part = dot3(c_w9[...], flat)
-    zi = iota((128, 128), 0)
-    lane = iota((128, 128), 1)
-    slot = lane & 15
-    place = jnp.where(((lane >> 4) == gz) & (slot < 10), composite4(zi, slot - 1), 0.0)
-    tx1[...] = dot3(part, place)
-    rx1[0] = tx1[...]
+    loads = [
+        pltpu.make_async_copy(source, target, load_sem.at[n])
+        for n, (source, target) in enumerate(
+            [
+                (charges, ext.at[pl.ds(8, 16), pl.ds(8, 16), :]),
+                (table_in, table),
+                (exps_in, exps),
+                (amps_in, amps),
+                (top_x_in, top_x),
+                (top_y_in, top_y),
+                (top_z_in, top_z),
+            ]
+        )
+    ]
+    for load in loads:
+        load.start()
     pl.semaphore_wait(barrier, len(partners))
 
     def remote(src, dst, send, recv, where):
@@ -156,19 +170,36 @@
             for o in range(1, sizes[step])
         ]
 
-    source_a = {-1: pl.ds(8, 8), 0: pl.ds(8, 16), 1: pl.ds(16, 8)}
+    source_a = {-1: pl.ds(0, 8), 0: pl.ds(0, 16), 1: pl.ds(8, 8)}
     target_a = {-1: pl.ds(24, 8), 0: pl.ds(8, 16), 1: pl.ds(0, 8)}
-    copies_t1 = top_copies(0, tx1, rx1)
     copies_a = [
         remote(
-            ext.at[source_a[dx], source_a[dy], :], ext.at[target_a[dx], target_a[dy], :],
+            charges.at[source_a[dx], source_a[dy], :], ext.at[target_a[dx], target_a[dy], :],
             a_send.at[n], a_recv.at[n], (dx, dy, 0),
         )
         for n, (dx, dy) in enumerate(NEAR)
     ]
+    for copy in copies_a:
+        copy.start()
+
+    for load in loads:
+        load.wait()
+    own = ext[8:24, 8:24, :]
+    c_rt, c_r = table[256:384, 0:128], table[256:384, 128:256]
+    c_edge, c_ry, c_sel = table[384:416, 0:128], table[384:408, 128:192], table[416:432, 0:128]
+
+    flat_h, flat_l = split(own.reshape(256, 128))
+    w9_h, w9_l = table[432:448, :], table[448:464, :]
+    part = dot(w9_h, flat_h) + dot(w9_h, flat_l) + dot(w9_l, flat_h)
+    zi = iota((128, 128), 0)
+    lane = iota((128, 128), 1)
+    slot = lane & 15
+    place = jnp.where(((lane >> 4) == gz) & (slot < 10), composite4(zi, slot - 1), 0.0)
+    tx1[...] = dot3(part, place)
+    rx1[0] = tx1[...]
+
+    copies_t1 = top_copies(0, tx1, rx1)
     for copy in copies_t1:
-        copy.start()
-    for copy in copies_a:
         copy.start()
 
     for level in range(2):
@@ -225,14 +256,15 @@
         valid = ((rr >> 2) < 3) & ((rr & 3) < 3) & (((ll & 15) >> 2) < 3) & ((ll & 3) < 3)
         return jnp.where(same & valid, whole, 0.0)
 
+    zi = iota((128, 128), 0)
+    zo = iota((128, 128), 1)
+    band_z0 = jnp.concatenate([band(0, r, zi - zo) for r in range(TERMS)], axis=0)
+    h_row = iota((16, 128), 0)
+    h_lane = iota((16, 128), 1)
+    h_out = jnp.where(h_row < 8, h_row - 8, h_row + 120)
+    edge_z0 = jnp.concatenate([band(0, r, h_lane - h_out) for r in range(TERMS)], axis=1)
     mix_x = tops(top_x[...], gx, sizes, True)
-    for n, copy in enumerate(copies_t1):
-        copy.wait_recv()
-    tx2[...] = dot3(mix_x, rx1[...].reshape(128, 128))
-    rx2[0] = tx2[...]
-    copies_t2 = top_copies(1, tx2, rx2)
-    for copy in copies_t2:
-        copy.start()
+    mix_y = tops(top_y[...], gy, sizes, False)
 
     for copy in copies_a:
         copy.wait_recv()
@@ -240,7 +272,7 @@
     for i in range(10):
         rx = 0.25 * (ext[2 * i + 5] + ext[2 * i + 8]) + 0.75 * (ext[2 * i + 6] + ext[2 * i + 7])
         hi, lo = split(rx)
-        cells = dot(c_ry[...], jnp.concatenate([hi, lo], axis=0))
+        cells = dot(c_ry, jnp.concatenate([hi, lo], axis=0))
         fext[8 + i, 8:24, :] = cells[0:16]
         q2[i] = cells[16:24]
 
@@ -259,14 +291,36 @@
     for copy in copies_b:
         copy.start()
 
-    mix_y = tops(top_y[...], gy, sizes, False)
+    for n, copy in enumerate(copies_t1):
+        copy.wait_recv()
+    tx2[...] = dot3(mix_x, rx1[...].reshape(128, 128))
+    rx2[0] = tx2[...]
+    copies_t2 = top_copies(1, tx2, rx2)
     for copy in copies_t2:
-        copy.wait_recv()
-    tx3[...] = dot3(mix_y, rx2[...].reshape(128, 128))
-    rx3[0] = tx3[...]
-    copies_t3 = top_copies(2, tx3, rx3)
-    for copy in copies_t3:
-        copy.start()
+        copy.start()
+
+    g_row = iota((32, 128), 0)
+    g_cell = iota((32, 128), 1) - 1
+    g_out = jnp.where(g_row < 16, g_row - 9, g_row + 47)
+    g_out = jnp.where((g_row & 15) < 10, g_out, 1000)
+    mains, edges = [], []
+    for r in range(TERMS):
+        gh, gl = split(band(1, r, zi - zo))
+        ch, cl = split(dot(c_r, gh) + dot(c_r, gl))
+        mains.append(dot(ch, c_rt) + dot(cl, c_rt))
+        eh, el = split(band(1, r, g_cell - g_out))
+        edges.append(dot(eh, c_rt) + dot(el, c_rt))
+    main_h, main_l = split(jnp.concatenate(mains, axis=0))
+    edge_h, edge_l = split(jnp.concatenate(edges, axis=1))
+
+    p_at = iota((128, 64), 1)
+    z_at = iota((128, 64), 0)
+    cell = ((p_at - 8 * gz + 65) & 63) - 1
+    spread = jnp.where(cell <= 8, composite4(z_at, cell), 0.0)
+    q_at = iota((64, 128), 0)
+    k_at = iota((64, 128), 1)
+    picked = jnp.where((q_at == ((8 * (k_at >> 4) + (k_at & 15) + 63) & 63)) & ((k_at & 15) < 10), 1.0, 0.0)
+    top_mix = dot3(dot3(spread, top_z[...]), picked)
 
     def smooth_y(source, band_y, target, at_x):
         hi, lo = split(source[at_x])
@@ -292,13 +346,6 @@
 
     smooth_x(v0, y0, 0, 16, 16)
 
-    zi = iota((128, 128), 0)
-    zo = iota((128, 128), 1)
-    band_z0 = jnp.concatenate([band(0, r, zi - zo) for r in range(TERMS)], axis=0)
-    h_row = iota((16, 128), 0)
-    h_lane = iota((16, 128), 1)
-    h_out = jnp.where(h_row < 8, h_row - 8, h_row + 120)
-    edge_z0 = jnp.concatenate([band(0, r, h_lane - h_out) for r in range(TERMS)], axis=1)
     y0h, y0l = split(y0[...])
     eh, el = split(edge_z0)
     nt = ((1,), (1,))
@@ -313,28 +360,13 @@
     bh, bl = split(band_z0)
     out[...] = (dot(y0h, bh) + dot(y0h, bl) + dot(y0l, bh)).reshape(16, 16, 128)
 
-    g_row = iota((32, 128), 0)
-    g_cell = iota((32, 128), 1) - 1
-    g_out = jnp.where(g_row < 16, g_row - 9, g_row + 47)
-    g_out = jnp.where((g_row & 15) < 10, g_out, 1000)
-    mains, edges = [], []
-    for r in range(TERMS):
-        gh, gl = split(band(1, r, zi - zo))
-        ch, cl = split(dot(c_r[...], gh) + dot(c_r[...], gl))
-        mains.append(dot(ch, c_rt[...]) + dot(cl, c_rt[...]))
-        eh, el = split(band(1, r, g_cell - g_out))
-        edges.append(dot(eh, c_rt[...]) + dot(el, c_rt[...]))
-    main_h, main_l = split(jnp.concatenate(mains, axis=0))
-    edge_h, edge_l = split(jnp.concatenate(edges, axis=1))
-
-    p_at = iota((128, 64), 1)
-    z_at = iota((128, 64), 0)
-    cell = ((p_at - 8 * gz + 65) & 63) - 1
-    spread = jnp.where(cell <= 8, composite4(z_at, cell), 0.0)
-    q_at = iota((64, 128), 0)
-    k_at = iota((64, 128), 1)
-    picked = jnp.where((q_at == ((8 * (k_at >> 4) + (k_at & 15) + 63) & 63)) & ((k_at & 15) < 10), 1.0, 0.0)
-    top_mix = dot3(dot3(spread, top_z[...]), picked)
+    for copy in copies_t2:
+        copy.wait_recv()
+    tx3[...] = dot3(mix_y, rx2[...].reshape(128, 128))
+    rx3[0] = tx3[...]
+    copies_t3 = top_copies(2, tx3, rx3)
+    for copy in copies_t3:
+        copy.start()
 
     for copy in copies_b:
         copy.wait_recv()
@@ -362,20 +394,22 @@
     total = rx3[0]
     for o in range(1, nz):
         total = total + rx3[o]
-    level1 = level1 + dot3(c_p3[...], dot3(total, top_mix, nt))
+    top_h, top_l = split(dot3(total, top_mix, nt))
 
     for copy in copies_z0:
         copy.wait_recv()
     tn = ((0,), (0,))
     zh, zl = split(zr0[...])
-    potential = out[...].reshape(256, 128) + dot(zh, c_sel[...], tn) + dot(zl, c_sel[...], tn)
+    potential = out[...].reshape(256, 128) + dot(zh, c_sel, tn) + dot(zl, c_sel, tn)
     for copy in copies_z1:
         copy.wait_recv()
     zh, zl = split(zr1[...])
-    side = dot(zh, c_edge[...], tn) + dot(zl, c_edge[...], tn)
+    side = dot(zh, c_edge, tn) + dot(zl, c_edge, tn)
     level1 = level1 + side[0:160]
     lh, ll = split(level1)
-    out[...] = (potential + dot(c_pp[...], lh) + dot(c_pp[...], ll)).reshape(16, 16, 128)
+    potential = potential + dot(table[0:256, 0:192], jnp.concatenate([lh, top_h, top_h], axis=0))
+    potential = potential + dot(table[0:256, 0:176], jnp.concatenate([ll, top_l], axis=0))
+    out[...] = potential.reshape(16, 16, 128)
 
     for copy in copies_t1 + copies_a + copies_t2 + copies_b + copies_t3 + copies_z0 + copies_z1:
         copy.wait_send()
@@ -383,17 +417,24 @@
 
 def solution(mesh):
     sizes = tuple(mesh.shape[axis] for axis in AXES)
-    consts = tables()
+    packed = tables()
 
     def local(charges, exponents, amplitudes, top_x, top_y, top_z):
         vmem = pl.BlockSpec(memory_space=pltpu.VMEM)
-        smem = pl.BlockSpec(memory_space=pltpu.SMEM)
+        hbm = pl.BlockSpec(memory_space=pltpu.HBM)
         return pl.pallas_call(
             functools.partial(kernel, sizes),
             out_shape=jax.ShapeDtypeStruct(charges.shape, F32),
-            in_specs=[vmem, smem, smem, vmem, vmem, vmem] + [vmem] * len(consts),
+            in_specs=[hbm] * 7,
             out_specs=vmem,
             scratch_shapes=[
+                pltpu.SMEM((2, TERMS), F32),
+                pltpu.SMEM((2, TERMS), F32),
+                pltpu.VMEM(top_x.shape, F32),
+                pltpu.VMEM(top_y.shape, F32),
+                pltpu.VMEM(top_z.shape, F32),
+                pltpu.VMEM(packed.shape, BF16),
+                pltpu.SemaphoreType.DMA((7,)),
                 pltpu.VMEM((32, 32, 128), F32),
                 pltpu.VMEM((32, 64, 128), F32),
                 pltpu.VMEM((256, 512), F32),
@@ -425,7 +466,10 @@
             compiler_params=pltpu.CompilerParams(
                 collective_id=0, has_side_effects=True, vmem_limit_bytes=40 * 2**20
             ),
-        )(charges, exponents, amplitudes, top_x, top_y, top_z, *[jnp.asarray(c) for c in consts])
+        )(*[
+            pltpu.with_memory_space_constraint(v, pltpu.HBM)
+            for v in (charges, exponents, amplitudes, top_x, top_y, top_z, jnp.asarray(packed))
+        ])
 
     in_specs = (P("gx", "gy", "gz"), P(), P(), P(), P(), P())
     return jax.shard_map(local, mesh=mesh, in_specs=in_specs, out_specs=P("gx", "gy", "gz"), check_vma=False)

time: 47.1 us -> 35.7 us (0.76)
  local copies, waits for them, and re-layouts: 10.5 us -> 0.66 us
  Pallas kernels: 36 us -> 34.8 us
    unnamed x29 -> x1, local copies, waits for them, and re-layouts: 10.5 us -> 0.66 us
    pallas_call x1, Pallas kernels: 36 us -> 34.8 us  [local(): pl.pallas_call(functools.partial(kernel, sizes), out_shape=jax.ShapeDtype...]
where the time goes in v2:
time: 35.7 us; the launch traced here: 35.5 us
  Pallas kernels  34.8 us (97%)
  local copies, waits for them, and re-layouts  0.66 us (2%)
    pallas_call x1, Pallas kernels, local(): pl.pallas_call(functools.partial(kernel, sizes), out_shape=jax.ShapeDtype...  34.8 us

profile of v2, /device:TPU:1, one launch (start us, length us, event | category | flops | bytes accessed | tf_op | source)
XLA Modules:
  0.0 35.5 jit_solution(3167437121048951845)
XLA Ops:
  0.0 34.8 %shard_map.73 = f32[16,16,128]{2,1,0:T(8,128)S(1)} custom-call(f32[16,16,128]{2,1,0:T(8,128)} %charges.1, f32[2,4]{1,0:T(2,128)} %exps_in.1, f32[2,4]{1,0:T(2,128)} %amps_in.1, f32[8,8]{1,0:T(8,128)} %top_x_in.1, f32[8,8]{1,0:T(8,128)} %top_y_in.1, f32[64,64]{1,0:T(8,128)} %top_z_in.1, bf16[464,256]{1,0:T(8,128)(2,1)} %constant.2.clone.table_in), custom_call_target="tpu_custom_call" | custom-call | tf_op jit(solution)/shard_map/pallas_call | solution.py:425
  34.8 0.7 %copy.9 = f32[16,16,128]{2,1,0:T(8,128)} copy(f32[16,16,128]{2,1,0:T(8,128)S(1)} %shard_map.73) | data formatting | bytes 262144

commit v3 on v2

--- a/solution.py
+++ b/solution.py
@@ -13,7 +13,7 @@
 REACH = 8
 F32 = jnp.float32
 BF16 = jnp.bfloat16
-NEAR = [(dx, dy) for dx in (-1, 0, 1) for dy in (-1, 0, 1) if (dx, dy) != (0, 0)]
+NEAR = [(dx, dy) for dx in (-1, 1) for dy in (-1, 1)] + [(-1, 0), (1, 0), (0, -1), (0, 1)]
 AXES = ("gx", "gy", "gz")
 
 
@@ -61,10 +61,17 @@
     sel = (zf == np.where(t < 8, 120 + t, t - 8)).astype(np.float64)
     bf = lambda v: np.asarray(v, np.float32).astype(jnp.bfloat16)
     lo = lambda v: np.asarray(v, np.float32) - bf(v).astype(np.float32)
-    packed = np.zeros((464, 256), jnp.bfloat16)
+    lanes = np.arange(128)
+    lane_a, lane_b, lane_c = lanes // 30, lanes // 10 % 3, lanes % 10
+    place = composite_at(4, np.arange(128)[:, None], lane_c[None, :] - 1) * (lanes < 90)
+    own_row = (np.arange(16)[:, None] == (lane_a * 4 + lane_b)[None, :]) & (lanes < 90)
+    packed = np.zeros((592, 256), jnp.bfloat16)
+    packed[464:592, 0:128] = bf(place)
+    packed[416:432, 128:256] = bf(own_row)
     packed[0:256, 0:160] = bf(pp)
     packed[0:256, 160:176] = bf(p4)
     packed[0:256, 176:192] = bf(lo(p4))
+    packed[0:256, 192:208] = bf(p4)
     packed[256:384, 0:128] = bf(rt)
     packed[256:384, 128:256] = bf(rt.T)
     packed[384:416, 0:128] = bf(edge)
@@ -117,7 +124,7 @@
     out,
     exps, amps, top_x, top_y, top_z, table, load_sem,
     ext, v0, y0, fext, q2, v1, y1,
-    rx1, rx2, rx3, tx1, tx2, tx3,
+    rx1, rx2, rx3,
     zs0, zs1, zr0, zr1,
     taps, inv,
     a_send, a_recv, b_send, b_recv, t_send, t_recv, z_send, z_recv,
@@ -153,7 +160,6 @@
     ]
     for load in loads:
         load.start()
-    pl.semaphore_wait(barrier, len(partners))
 
     def remote(src, dst, send, recv, where):
         return pltpu.make_async_remote_copy(
@@ -170,6 +176,21 @@
             for o in range(1, sizes[step])
         ]
 
+    for load in loads[:2]:
+        load.wait()
+    own = ext[8:24, 8:24, :]
+    c_rt, c_r = table[256:384, 0:128], table[256:384, 128:256]
+    c_edge, c_ry, c_sel = table[384:416, 0:128], table[384:408, 128:192], table[416:432, 0:128]
+
+    flat_h, flat_l = split(own.reshape(256, 128))
+    w9_h, w9_l = table[432:448, :], table[448:464, :]
+    part = dot(w9_h, flat_h) + dot(w9_h, flat_l) + dot(w9_l, flat_h)
+    part_h, part_l = split(part)
+    place = table[464:592, 0:128]
+    placed = (dot(part_h, place) + dot(part_l, place)) * table[416:432, 128:256].astype(F32)
+    rx1[0] = jnp.sum(placed, axis=0, keepdims=True)
+
+    pl.semaphore_wait(barrier, len(partners))
     source_a = {-1: pl.ds(0, 8), 0: pl.ds(0, 16), 1: pl.ds(8, 8)}
     target_a = {-1: pl.ds(24, 8), 0: pl.ds(8, 16), 1: pl.ds(0, 8)}
     copies_a = [
@@ -182,25 +203,12 @@
     for copy in copies_a:
         copy.start()
 
-    for load in loads:
+    copies_t1 = top_copies(0, rx1.at[0], rx1)
+    for copy in copies_t1:
+        copy.start()
+
+    for load in loads[2:]:
         load.wait()
-    own = ext[8:24, 8:24, :]
-    c_rt, c_r = table[256:384, 0:128], table[256:384, 128:256]
-    c_edge, c_ry, c_sel = table[384:416, 0:128], table[384:408, 128:192], table[416:432, 0:128]
-
-    flat_h, flat_l = split(own.reshape(256, 128))
-    w9_h, w9_l = table[432:448, :], table[448:464, :]
-    part = dot(w9_h, flat_h) + dot(w9_h, flat_l) + dot(w9_l, flat_h)
-    zi = iota((128, 128), 0)
-    lane = iota((128, 128), 1)
-    slot = lane & 15
-    place = jnp.where(((lane >> 4) == gz) & (slot < 10), composite4(zi, slot - 1), 0.0)
-    tx1[...] = dot3(part, place)
-    rx1[0] = tx1[...]
-
-    copies_t1 = top_copies(0, tx1, rx1)
-    for copy in copies_t1:
-        copy.start()
 
     for level in range(2):
         for r in range(TERMS):
@@ -237,25 +245,6 @@
     off1 = jnp.where((row & 15) < 10, where1 - ((row & 15) - 1), 1000)
     band_y1 = tripled(band(1, row >> 4, off1), col >> 5)
 
-    def tops(table, own, shape_sizes, first):
-        r8 = iota((16, 8), 0)
-        p8 = iota((16, 8), 1)
-        c8 = iota((8, 128), 0)
-        l8 = iota((8, 128), 1)
-        rr = iota((16, 128), 0)
-        ll = iota((16, 128), 1)
-        if first:
-            mine, theirs = r8 >> 2, (l8 & 15) >> 2
-            same = (rr & 3) == (ll & 3)
-        else:
-            mine, theirs = r8 & 3, l8 & 3
-            same = (rr >> 2) == ((ll & 15) >> 2)
-        pick_rows = (p8 == ((own + mine + 7) & 7)).astype(F32)
-        pick_cols = (c8 == ((own - (l8 >> 4) + theirs + 15) & 7)).astype(F32)
-        whole = dot3(dot3(pick_rows, table), pick_cols)
-        valid = ((rr >> 2) < 3) & ((rr & 3) < 3) & (((ll & 15) >> 2) < 3) & ((ll & 3) < 3)
-        return jnp.where(same & valid, whole, 0.0)
-
     zi = iota((128, 128), 0)
     zo = iota((128, 128), 1)
     band_z0 = jnp.concatenate([band(0, r, zi - zo) for r in range(TERMS)], axis=0)
@@ -263,8 +252,39 @@
     h_lane = iota((16, 128), 1)
     h_out = jnp.where(h_row < 8, h_row - 8, h_row + 120)
     edge_z0 = jnp.concatenate([band(0, r, h_lane - h_out) for r in range(TERMS)], axis=1)
-    mix_x = tops(top_x[...], gx, sizes, True)
-    mix_y = tops(top_y[...], gy, sizes, False)
+    slot_at = iota((8, 128), 0)
+    lane_at = iota((8, 128), 1)
+    tens = (lane_at * 205) >> 11
+    lane_a = (tens * 11) >> 5
+    lane_b = tens - 3 * lane_a
+
+    def top_weights(kernel_rows, own_at, lane_cell, extent):
+        source = (own_at - slot_at + lane_cell + extent - 1) & (extent - 1)
+        found = []
+        for shift in range(3):
+            row_at = lax.rem(own_at + shift + extent - 1, extent)
+            weights = jnp.zeros((8, 128), F32)
+            for q in range(extent):
+                weights = jnp.where(source == q, kernel_rows[row_at, q], weights)
+            found.append(weights)
+        return found
+
+    weights_x = top_weights(top_x, gx, lane_a, nx)
+    weights_y = top_weights(top_y, gy, lane_b, ny)
+
+    l16 = iota((16, 128), 1)
+    r16 = iota((16, 128), 0)
+    within = l16 - 30 * (r16 >> 2)
+    keep_top = (within >= 0) & (within < 10) & (r16 < 12) & ((r16 & 3) < 3)
+    from_lane = iota((128, 128), 0)
+    from_lane = from_lane - 30 * ((((from_lane * 205) >> 11) * 11) >> 5)
+    slot_z = jnp.where((from_lane < 10) & (iota((128, 128), 1) == 16 * gz + from_lane), 1.0, 0.0).astype(BF16)
+
+    def contracted(received, weights, step):
+        slots = received[...].reshape(8, 128)
+        sums = [jnp.sum(slots * w, axis=0, keepdims=True) for w in weights]
+        rows = jnp.where(slot_at == 0, sums[0], jnp.where(slot_at == 1, sums[1], sums[2]))
+        return rows + pltpu.roll(rows, 128 - step, 1) + pltpu.roll(rows, 128 - 2 * step, 1)
 
     for copy in copies_a:
         copy.wait_recv()
@@ -293,9 +313,10 @@
 
     for n, copy in enumerate(copies_t1):
         copy.wait_recv()
-    tx2[...] = dot3(mix_x, rx1[...].reshape(128, 128))
-    rx2[0] = tx2[...]
-    copies_t2 = top_copies(1, tx2, rx2)
+    folded = contracted(rx1, weights_x, 30)
+    spread_x = jnp.where(slot_at == 0, folded, jnp.where(slot_at == 1, pltpu.roll(folded, 30, 1), pltpu.roll(folded, 60, 1)))
+    rx2[0] = jnp.sum(jnp.where(lane_a == slot_at, spread_x, 0.0), axis=0, keepdims=True)
+    copies_t2 = top_copies(1, rx2.at[0], rx2)
     for copy in copies_t2:
         copy.start()
 
@@ -362,9 +383,13 @@
 
     for copy in copies_t2:
         copy.wait_recv()
-    tx3[...] = dot3(mix_y, rx2[...].reshape(128, 128))
-    rx3[0] = tx3[...]
-    copies_t3 = top_copies(2, tx3, rx3)
+    folded = contracted(rx2, weights_y, 10)
+    r16 = iota((16, 128), 0)
+    wide = jnp.where((r16 & 3) == 0, folded[0:1], jnp.where((r16 & 3) == 1, folded[1:2], folded[2:3]))
+    wide = jnp.where(keep_top, wide, 0.0)
+    wide_h, wide_l = split(wide)
+    rx3[0] = dot(wide_h, slot_z) + dot(wide_l, slot_z)
+    copies_t3 = top_copies(2, rx3.at[0], rx3)
     for copy in copies_t3:
         copy.start()
 
@@ -389,27 +414,30 @@
         copy.start()
     level1 = dot(y1h, main_h) + dot(y1h, main_l) + dot(y1l, main_h)
 
+    lh, ll = split(level1)
+    from_cells = table[0:256, 0:160]
+    potential = out[...].reshape(256, 128) + dot(from_cells, lh) + dot(from_cells, ll)
+
     for copy in copies_t3:
         copy.wait_recv()
     total = rx3[0]
     for o in range(1, nz):
         total = total + rx3[o]
     top_h, top_l = split(dot3(total, top_mix, nt))
+    potential = potential + dot(table[0:256, 160:208], jnp.concatenate([top_h, top_h, top_l], axis=0))
 
     for copy in copies_z0:
         copy.wait_recv()
     tn = ((0,), (0,))
     zh, zl = split(zr0[...])
-    potential = out[...].reshape(256, 128) + dot(zh, c_sel, tn) + dot(zl, c_sel, tn)
+    out[...] = (potential + dot(zh, c_sel, tn) + dot(zl, c_sel, tn)).reshape(16, 16, 128)
+
     for copy in copies_z1:
         copy.wait_recv()
     zh, zl = split(zr1[...])
     side = dot(zh, c_edge, tn) + dot(zl, c_edge, tn)
-    level1 = level1 + side[0:160]
-    lh, ll = split(level1)
-    potential = potential + dot(table[0:256, 0:192], jnp.concatenate([lh, top_h, top_h], axis=0))
-    potential = potential + dot(table[0:256, 0:176], jnp.concatenate([ll, top_l], axis=0))
-    out[...] = potential.reshape(16, 16, 128)
+    lh, ll = split(side[0:160])
+    out[...] = out[...] + (dot(from_cells, lh) + dot(from_cells, ll)).reshape(16, 16, 128)
 
     for copy in copies_t1 + copies_a + copies_t2 + copies_b + copies_t3 + copies_z0 + copies_z1:
         copy.wait_send()
@@ -430,8 +458,8 @@
             scratch_shapes=[
                 pltpu.SMEM((2, TERMS), F32),
                 pltpu.SMEM((2, TERMS), F32),
-                pltpu.VMEM(top_x.shape, F32),
-                pltpu.VMEM(top_y.shape, F32),
+                pltpu.SMEM(top_x.shape, F32),
+                pltpu.SMEM(top_y.shape, F32),
                 pltpu.VMEM(top_z.shape, F32),
                 pltpu.VMEM(packed.shape, BF16),
                 pltpu.SemaphoreType.DMA((7,)),
@@ -442,12 +470,9 @@
                 pltpu.VMEM((10, 8, 128), F32),
                 pltpu.VMEM((26, 64, 128), F32),
                 pltpu.VMEM((160, 512), F32),
+                pltpu.VMEM((8, 1, 128), F32),
+                pltpu.VMEM((8, 1, 128), F32),
                 pltpu.VMEM((8, 16, 128), F32),
-                pltpu.VMEM((8, 16, 128), F32),
-                pltpu.VMEM((8, 16, 128), F32),
-                pltpu.VMEM((16, 128), F32),
-                pltpu.VMEM((16, 128), F32),
-                pltpu.VMEM((16, 128), F32),
                 pltpu.VMEM((16, 256), F32),
                 pltpu.VMEM((32, 256), F32),
                 pltpu.VMEM((16, 256), F32),

time: 35.7 us -> 34.9 us (0.978)
  Pallas kernels: 34.8 us -> 34.1 us
    pallas_call x1, Pallas kernels: 34.8 us -> 34.1 us  [local(): pl.pallas_call(functools.partial(kernel, sizes), out_shape=jax.ShapeDtype...]
where the time goes in v3:
time: 34.9 us; the launch traced here: 34.7 us
  Pallas kernels  34.1 us (98%)
  local copies, waits for them, and re-layouts  0.66 us (2%)
    pallas_call x1, Pallas kernels, local(): pl.pallas_call(functools.partial(kernel, sizes), out_shape=jax.ShapeDtype...  34.1 us

profile of v3, /device:TPU:1, one launch (start us, length us, event | category | flops | bytes accessed | tf_op | source)
XLA Modules:
  0.0 34.7 jit_solution(15384563801317495402)
XLA Ops:
  0.0 34.1 %shard_map.73 = f32[16,16,128]{2,1,0:T(8,128)S(1)} custom-call(f32[16,16,128]{2,1,0:T(8,128)} %charges.1, f32[2,4]{1,0:T(2,128)} %exps_in.1, f32[2,4]{1,0:T(2,128)} %amps_in.1, f32[8,8]{1,0:T(8,128)} %top_x_in.1, f32[8,8]{1,0:T(8,128)} %top_y_in.1, f32[64,64]{1,0:T(8,128)} %top_z_in.1, bf16[592,256]{1,0:T(8,128)(2,1)} %constant.2.clone.table_in), custom_call_target="tpu_custom_call" | custom-call | tf_op jit(solution)/shard_map/pallas_call | solution.py:453
  34.1 0.7 %copy.9 = f32[16,16,128]{2,1,0:T(8,128)} copy(f32[16,16,128]{2,1,0:T(8,128)S(1)} %shard_map.73) | data formatting | bytes 262144

commit v4 on v3

--- a/solution.py
+++ b/solution.py
@@ -82,6 +82,11 @@
     return packed
 
 
+def offsets(count, odd_far=False):
+    ring = lambda o: min(o, count - o)
+    return sorted(range(1, count), key=lambda o: (-(o % 2) if odd_far else 0, -ring(o)))
+
+
 def split(v):
     hi = v.astype(BF16)
     return hi, (v - hi.astype(F32)).astype(BF16)
@@ -123,7 +128,7 @@
     charges, exps_in, amps_in, top_x_in, top_y_in, top_z_in, table_in,
     out,
     exps, amps, top_x, top_y, top_z, table, load_sem,
-    ext, v0, y0, fext, q2, v1, y1,
+    ext, v0, y0, fext, q2, q3, edge_rows, v1, y1,
     rx1, rx2, rx3,
     zs0, zs1, zr0, zr1,
     taps, inv,
@@ -136,10 +141,10 @@
     def at(dx, dy, dz):
         return (lax.rem(gx + dx + nx, nx), lax.rem(gy + dy + ny, ny), lax.rem(gz + dz + nz, nz))
 
-    partners = [(dx, dy, 0) for dx, dy in NEAR]
-    partners += [(o, 0, 0) for o in range(2, nx - 1)]
-    partners += [(0, o, 0) for o in range(2, ny - 1)]
-    partners += [(0, 0, o) for o in range(1, nz)]
+    partners = [(0, 0, o) for o in offsets(nz, True)]
+    partners += [(o, 0, 0) for o in offsets(nx) if 1 < o < nx - 1]
+    partners += [(0, o, 0) for o in offsets(ny) if 1 < o < ny - 1]
+    partners += [(dx, dy, 0) for dx, dy in NEAR]
     barrier = pltpu.get_barrier_semaphore()
     for p in partners:
         pl.semaphore_signal(barrier, inc=1, device_id=at(*p), device_id_type=MESH)
@@ -173,9 +178,11 @@
                 src, dst.at[o], t_send.at[step * 8 + o], t_recv.at[step * 8 + o],
                 (shift[0] * o, shift[1] * o, shift[2] * o),
             )
-            for o in range(1, sizes[step])
+            for o in offsets(sizes[step], step == 2)
         ]
 
+    zs1[...] = jnp.zeros_like(zs1)
+    edge_rows[:, 16:24, :] = jnp.zeros((2, 8, 128), F32)
     for load in loads[:2]:
         load.wait()
     own = ext[8:24, 8:24, :]
@@ -191,20 +198,33 @@
     rx1[0] = jnp.sum(placed, axis=0, keepdims=True)
 
     pl.semaphore_wait(barrier, len(partners))
-    source_a = {-1: pl.ds(0, 8), 0: pl.ds(0, 16), 1: pl.ds(8, 8)}
-    target_a = {-1: pl.ds(24, 8), 0: pl.ds(8, 16), 1: pl.ds(0, 8)}
-    copies_a = [
-        remote(
-            charges.at[source_a[dx], source_a[dy], :], ext.at[target_a[dx], target_a[dy], :],
-            a_send.at[n], a_recv.at[n], (dx, dy, 0),
-        )
-        for n, (dx, dy) in enumerate(NEAR)
-    ]
-    for copy in copies_a:
-        copy.start()
+    source_x = {-1: [(0, 3), (3, 5)], 0: [(0, 16)], 1: [(13, 3), (8, 5)]}
+    target_x = {-1: [24, 27], 0: [8], 1: [5, 0]}
+    source_y = {-1: (0, 8), 0: (0, 16), 1: (8, 8)}
+    target_y = {-1: 24, 0: 8, 1: 0}
+
+    def halo_copies(part):
+        found = []
+        for n, (dx, dy) in enumerate(NEAR):
+            if part < len(source_x[dx]):
+                start, size = source_x[dx][part]
+                start_y, size_y = source_y[dy]
+                found.append(
+                    remote(
+                        charges.at[pl.ds(start, size), pl.ds(start_y, size_y), :],
+                        ext.at[pl.ds(target_x[dx][part], size), pl.ds(target_y[dy], size_y), :],
+                        a_send.at[part * 8 + n], a_recv.at[part * 8 + n], (dx, dy, 0),
+                    )
+                )
+        return found
 
     copies_t1 = top_copies(0, rx1.at[0], rx1)
     for copy in copies_t1:
+        copy.start()
+    copies_a, copies_far = halo_copies(0), halo_copies(1)
+    for copy in copies_a:
+        copy.start()
+    for copy in copies_far:
         copy.start()
 
     for load in loads[2:]:
@@ -286,6 +306,15 @@
         rows = jnp.where(slot_at == 0, sums[0], jnp.where(slot_at == 1, sums[1], sums[2]))
         return rows + pltpu.roll(rows, 128 - step, 1) + pltpu.roll(rows, 128 - 2 * step, 1)
 
+    for n, copy in enumerate(copies_t1):
+        copy.wait_recv()
+    folded = contracted(rx1, weights_x, 30)
+    spread_x = jnp.where(slot_at == 0, folded, jnp.where(slot_at == 1, pltpu.roll(folded, 30, 1), pltpu.roll(folded, 60, 1)))
+    rx2[0] = jnp.sum(jnp.where(lane_a == slot_at, spread_x, 0.0), axis=0, keepdims=True)
+    copies_t2 = top_copies(1, rx2.at[0], rx2)
+    for copy in copies_t2:
+        copy.start()
+
     for copy in copies_a:
         copy.wait_recv()
 
@@ -295,29 +324,28 @@
         cells = dot(c_ry, jnp.concatenate([hi, lo], axis=0))
         fext[8 + i, 8:24, :] = cells[0:16]
         q2[i] = cells[16:24]
+        if i < 8:
+            q3[1, 2 * i : 2 * i + 2, :] = cells[8:10]
+        if i >= 2:
+            q3[0, 2 * i - 4 : 2 * i - 2, :] = cells[8:10]
 
     xs = {-1: pl.ds(10, 8), 0: pl.ds(8, 10), 1: pl.ds(8, 8)}
     xd = {-1: pl.ds(18, 8), 0: pl.ds(8, 10), 1: pl.ds(0, 8)}
-    yd = {-1: pl.ds(24, 8), 0: pl.ds(8, 16), 1: pl.ds(0, 8)}
+    yd = {-1: pl.ds(24, 8), 0: pl.ds(8, 8), 1: pl.ds(0, 8)}
     copies_b = []
     for n, (dx, dy) in enumerate(NEAR):
         if dy == -1:
             src = q2.at[pl.ds(xs[dx].start - 8, xs[dx].size)]
         else:
-            src = fext.at[xs[dx], pl.ds(8, 16 if dy == 0 else 8), :]
+            src = fext.at[xs[dx], pl.ds(8, 8), :]
         copies_b.append(
             remote(src, fext.at[xd[dx], yd[dy], :], b_send.at[n], b_recv.at[n], (dx, dy, 0))
         )
+    for side, dx in enumerate((-1, 1)):
+        copies_b.append(
+            remote(q3.at[side], edge_rows.at[side, pl.ds(0, 16)], b_send.at[8 + side], b_recv.at[8 + side], (dx, 0, 0))
+        )
     for copy in copies_b:
-        copy.start()
-
-    for n, copy in enumerate(copies_t1):
-        copy.wait_recv()
-    folded = contracted(rx1, weights_x, 30)
-    spread_x = jnp.where(slot_at == 0, folded, jnp.where(slot_at == 1, pltpu.roll(folded, 30, 1), pltpu.roll(folded, 60, 1)))
-    rx2[0] = jnp.sum(jnp.where(lane_a == slot_at, spread_x, 0.0), axis=0, keepdims=True)
-    copies_t2 = top_copies(1, rx2.at[0], rx2)
-    for copy in copies_t2:
         copy.start()
 
     g_row = iota((32, 128), 0)
@@ -343,6 +371,9 @@
     picked = jnp.where((q_at == ((8 * (k_at >> 4) + (k_at & 15) + 63) & 63)) & ((k_at & 15) < 10), 1.0, 0.0)
     top_mix = dot3(dot3(spread, top_z[...]), picked)
 
+    for copy in copies_far:
+        copy.wait_recv()
+
     def smooth_y(source, band_y, target, at_x):
         hi, lo = split(source[at_x])
         target[at_x] = dot(band_y, jnp.concatenate([hi, hi, lo], axis=0))
@@ -393,19 +424,27 @@
     for copy in copies_t3:
         copy.start()
 
-    for copy in copies_b:
-        copy.wait_recv()
-
-    def level1_y(step, carry):
-        for u in range(13):
-            smooth_y(fext, band_y1, v1, step * 13 + u)
-        return carry
-
-    lax.fori_loop(0, 2, level1_y, 0)
+    for group in (0, 1, -1):
+        for copy, (dx, dy) in zip(copies_b, NEAR + [(-1, 0), (1, 0)]):
+            if dx == group:
+                copy.wait_recv()
+        first = xd[group].start
+        if group != 0:
+            for x in range(8):
+                rows = edge_rows[0 if group == -1 else 1, 2 * x : 2 * x + 8, :]
+                fext[first + x, 16:24, :] = jnp.where(slot_at < 2, rows, 0.0)
+        half = xd[group].size // 2
+
+        def level1_y(step, carry, first=first, half=half):
+            for u in range(half):
+                smooth_y(fext, band_y1, v1, first + step * half + u)
+            return carry
+
+        lax.fori_loop(0, 2, level1_y, 0)
+
     smooth_x(v1, y1, 1, 10, 16)
     y1h, y1l = split(y1[...])
     zs1[:, 0:160] = dot(edge_h, y1h, nt) + dot(edge_h, y1l, nt) + dot(edge_l, y1h, nt)
-    zs1[:, 160:256] = jnp.zeros((32, 96), F32)
     copies_z1 = [
         remote(zs1.at[pl.ds(0, 16)], zr1.at[pl.ds(0, 16)], z_send.at[2], z_recv.at[2], left),
         remote(zs1.at[pl.ds(16, 16)], zr1.at[pl.ds(16, 16)], z_send.at[3], z_recv.at[3], right),
@@ -418,28 +457,27 @@
     from_cells = table[0:256, 0:160]
     potential = out[...].reshape(256, 128) + dot(from_cells, lh) + dot(from_cells, ll)
 
+    for copy in copies_z0:
+        copy.wait_recv()
+    tn = ((0,), (0,))
+    zh, zl = split(zr0[...])
+    out[...] = (potential + dot(zh, c_sel, tn) + dot(zl, c_sel, tn)).reshape(16, 16, 128)
+
     for copy in copies_t3:
         copy.wait_recv()
     total = rx3[0]
     for o in range(1, nz):
         total = total + rx3[o]
     top_h, top_l = split(dot3(total, top_mix, nt))
-    potential = potential + dot(table[0:256, 160:208], jnp.concatenate([top_h, top_h, top_l], axis=0))
-
-    for copy in copies_z0:
-        copy.wait_recv()
-    tn = ((0,), (0,))
-    zh, zl = split(zr0[...])
-    out[...] = (potential + dot(zh, c_sel, tn) + dot(zl, c_sel, tn)).reshape(16, 16, 128)
 
     for copy in copies_z1:
         copy.wait_recv()
     zh, zl = split(zr1[...])
-    side = dot(zh, c_edge, tn) + dot(zl, c_edge, tn)
-    lh, ll = split(side[0:160])
-    out[...] = out[...] + (dot(from_cells, lh) + dot(from_cells, ll)).reshape(16, 16, 128)
-
-    for copy in copies_t1 + copies_a + copies_t2 + copies_b + copies_t3 + copies_z0 + copies_z1:
+    side_h, side_l = split((dot(zh, c_edge, tn) + dot(zl, c_edge, tn))[0:160])
+    late = dot(table[0:256, 0:208], jnp.concatenate([side_h, top_h, top_h, top_l], axis=0)) + dot(from_cells, side_l)
+    out[...] = out[...] + late.reshape(16, 16, 128)
+
+    for copy in copies_t1 + copies_a + copies_far + copies_t2 + copies_b + copies_t3 + copies_z0 + copies_z1:
         copy.wait_send()
 
 
@@ -468,6 +506,8 @@
                 pltpu.VMEM((256, 512), F32),
                 pltpu.VMEM((26, 32, 128), F32),
                 pltpu.VMEM((10, 8, 128), F32),
+                pltpu.VMEM((2, 16, 128), F32),
+                pltpu.VMEM((2, 24, 128), F32),
                 pltpu.VMEM((26, 64, 128), F32),
                 pltpu.VMEM((160, 512), F32),
                 pltpu.VMEM((8, 1, 128), F32),
@@ -479,10 +519,10 @@
                 pltpu.VMEM((32, 256), F32),
                 pltpu.VMEM((72, 8, 128), F32),
                 pltpu.VMEM((8, 8, 128), F32),
-                pltpu.SemaphoreType.DMA((8,)),
-                pltpu.SemaphoreType.DMA((8,)),
-                pltpu.SemaphoreType.DMA((8,)),
-                pltpu.SemaphoreType.DMA((8,)),
+                pltpu.SemaphoreType.DMA((16,)),
+                pltpu.SemaphoreType.DMA((16,)),
+                pltpu.SemaphoreType.DMA((10,)),
+                pltpu.SemaphoreType.DMA((10,)),
                 pltpu.SemaphoreType.DMA((24,)),
                 pltpu.SemaphoreType.DMA((24,)),
                 pltpu.SemaphoreType.DMA((4,)),

time: 34.9 us -> 34.3 us (0.983)
  Pallas kernels: 34.1 us -> 33.5 us
    pallas_call x1, Pallas kernels: 34.1 us -> 33.5 us  [local(): pl.pallas_call(functools.partial(kernel, sizes), out_shape=jax.ShapeDtype...]
where the time goes in v4:
time: 34.3 us; the launch traced here: 34.2 us
  Pallas kernels  33.5 us (98%)
  local copies, waits for them, and re-layouts  0.66 us (2%)
    pallas_call x1, Pallas kernels, local(): pl.pallas_call(functools.partial(kernel, sizes), out_shape=jax.ShapeDtype...  33.5 us

profile of v4, /device:TPU:1, one launch (start us, length us, event | category | flops | bytes accessed | tf_op | source)
XLA Modules:
  0.0 34.2 jit_solution(14531590707431836439)
XLA Ops:
  0.0 33.5 %shard_map.73 = f32[16,16,128]{2,1,0:T(8,128)S(1)} custom-call(f32[16,16,128]{2,1,0:T(8,128)} %charges.1, f32[2,4]{1,0:T(2,128)} %exps_in.1, f32[2,4]{1,0:T(2,128)} %amps_in.1, f32[8,8]{1,0:T(8,128)} %top_x_in.1, f32[8,8]{1,0:T(8,128)} %top_y_in.1, f32[64,64]{1,0:T(8,128)} %top_z_in.1, bf16[592,256]{1,0:T(8,128)(2,1)} %constant.2.clone.table_in), custom_call_target="tpu_custom_call" | custom-call | tf_op jit(solution)/shard_map/pallas_call | solution.py:491
  33.5 0.7 %copy.9 = f32[16,16,128]{2,1,0:T(8,128)} copy(f32[16,16,128]{2,1,0:T(8,128)S(1)} %shard_map.73) | data formatting | bytes 262144

commit v5 on v4

--- a/solution.py
+++ b/solution.py
@@ -424,6 +424,9 @@
     for copy in copies_t3:
         copy.start()
 
+    for copy in copies_t1 + copies_a + copies_far + copies_t2:
+        copy.wait_send()
+
     for group in (0, 1, -1):
         for copy, (dx, dy) in zip(copies_b, NEAR + [(-1, 0), (1, 0)]):
             if dx == group:
@@ -463,6 +466,9 @@
     zh, zl = split(zr0[...])
     out[...] = (potential + dot(zh, c_sel, tn) + dot(zl, c_sel, tn)).reshape(16, 16, 128)
 
+    for copy in copies_b + copies_z0 + copies_t3 + copies_z1:
+        copy.wait_send()
+
     for copy in copies_t3:
         copy.wait_recv()
     total = rx3[0]
@@ -476,9 +482,6 @@
     side_h, side_l = split((dot(zh, c_edge, tn) + dot(zl, c_edge, tn))[0:160])
     late = dot(table[0:256, 0:208], jnp.concatenate([side_h, top_h, top_h, top_l], axis=0)) + dot(from_cells, side_l)
     out[...] = out[...] + late.reshape(16, 16, 128)
-
-    for copy in copies_t1 + copies_a + copies_far + copies_t2 + copies_b + copies_t3 + copies_z0 + copies_z1:
-        copy.wait_send()
 
 
 def solution(mesh):

time: 34.3 us -> 34.2 us (level)
  no operation moved by 1% of the time
where the time goes in v5:
time: 34.2 us; the launch traced here: 34.1 us
  Pallas kernels  33.5 us (98%)
  local copies, waits for them, and re-layouts  0.66 us (2%)
    pallas_call x1, Pallas kernels, local(): pl.pallas_call(functools.partial(kernel, sizes), out_shape=jax.ShapeDtype...  33.5 us

profile of v5, /device:TPU:1, one launch (start us, length us, event | category | flops | bytes accessed | tf_op | source)
XLA Modules:
  0.0 34.1 jit_solution(15477612130266670220)
XLA Ops:
  0.0 33.5 %shard_map.73 = f32[16,16,128]{2,1,0:T(8,128)S(1)} custom-call(f32[16,16,128]{2,1,0:T(8,128)} %charges.1, f32[2,4]{1,0:T(2,128)} %exps_in.1, f32[2,4]{1,0:T(2,128)} %amps_in.1, f32[8,8]{1,0:T(8,128)} %top_x_in.1, f32[8,8]{1,0:T(8,128)} %top_y_in.1, f32[64,64]{1,0:T(8,128)} %top_z_in.1, bf16[592,256]{1,0:T(8,128)(2,1)} %constant.2.clone.table_in), custom_call_target="tpu_custom_call" | custom-call | tf_op jit(solution)/shard_map/pallas_call | solution.py:494
  33.5 0.7 %copy.9 = f32[16,16,128]{2,1,0:T(8,128)} copy(f32[16,16,128]{2,1,0:T(8,128)S(1)} %shard_map.73) | data formatting | bytes 262144

commit v6 on v5

--- a/solution.py
+++ b/solution.py
@@ -385,8 +385,8 @@
 
     lax.fori_loop(0, 4, level0_y, 0)
 
-    def smooth_x(source, target, level, count, stride):
-        for r in range(TERMS):
+    def smooth_x(source, target, level, count, terms):
+        for r in terms:
             w = [taps[(level * TERMS + r) * 9 + k] for k in range(9)]
             for half in range(2):
                 rows = slice(r * 16 + half * 8, r * 16 + half * 8 + 8)
@@ -396,7 +396,7 @@
                         acc = acc + w[k] * (source[x + 8 - k, rows, :] + source[x + 8 + k, rows, :])
                     target[x * 16 + half * 8 : x * 16 + half * 8 + 8, r * 128 : r * 128 + 128] = acc
 
-    smooth_x(v0, y0, 0, 16, 16)
+    smooth_x(v0, y0, 0, 16, range(TERMS))
 
     y0h, y0l = split(y0[...])
     eh, el = split(edge_z0)
@@ -445,9 +445,16 @@
 
         lax.fori_loop(0, 2, level1_y, 0)
 
-    smooth_x(v1, y1, 1, 10, 16)
-    y1h, y1l = split(y1[...])
-    zs1[:, 0:160] = dot(edge_h, y1h, nt) + dot(edge_h, y1l, nt) + dot(edge_l, y1h, nt)
+    pairs, beyond = [], jnp.zeros((32, 160), F32)
+    for first in (0, 2):
+        smooth_x(v1, y1, 1, 10, (first, first + 1))
+        part = slice(first * 128, first * 128 + 256)
+        hi, lo = split(y1[:, part])
+        beyond = beyond + dot(edge_h[:, part], hi, nt) + dot(edge_h[:, part], lo, nt) + dot(edge_l[:, part], hi, nt)
+        pairs.append((hi, lo))
+    zs1[:, 0:160] = beyond
+    y1h = jnp.concatenate([hi for hi, _ in pairs], axis=1)
+    y1l = jnp.concatenate([lo for _, lo in pairs], axis=1)
     copies_z1 = [
         remote(zs1.at[pl.ds(0, 16)], zr1.at[pl.ds(0, 16)], z_send.at[2], z_recv.at[2], left),
         remote(zs1.at[pl.ds(16, 16)], zr1.at[pl.ds(16, 16)], z_send.at[3], z_recv.at[3], right),

time: 34.2 us -> 34.2 us (level)
  no operation moved by 1% of the time
where the time goes in v6:
time: 34.2 us; the launch traced here: 34.1 us
  Pallas kernels  33.4 us (98%)
  local copies, waits for them, and re-layouts  0.66 us (2%)
    pallas_call x1, Pallas kernels, local(): pl.pallas_call(functools.partial(kernel, sizes), out_shape=jax.ShapeDtype...  33.4 us

profile of v6, /device:TPU:1, one launch (start us, length us, event | category | flops | bytes accessed | tf_op | source)
XLA Modules:
  0.0 34.1 jit_solution(5458406747200532933)
XLA Ops:
  0.0 33.4 %shard_map.73 = f32[16,16,128]{2,1,0:T(8,128)S(1)} custom-call(f32[16,16,128]{2,1,0:T(8,128)} %charges.1, f32[2,4]{1,0:T(2,128)} %exps_in.1, f32[2,4]{1,0:T(2,128)} %amps_in.1, f32[8,8]{1,0:T(8,128)} %top_x_in.1, f32[8,8]{1,0:T(8,128)} %top_y_in.1, f32[64,64]{1,0:T(8,128)} %top_z_in.1, bf16[592,256]{1,0:T(8,128)(2,1)} %constant.2.clone.table_in), custom_call_target="tpu_custom_call" | custom-call | tf_op jit(solution)/shard_map/pallas_call | solution.py:501
  33.4 0.7 %copy.9 = f32[16,16,128]{2,1,0:T(8,128)} copy(f32[16,16,128]{2,1,0:T(8,128)S(1)} %shard_map.73) | data formatting | bytes 262144

commit v7 on v6

--- a/solution.py
+++ b/solution.py
@@ -141,14 +141,6 @@
     def at(dx, dy, dz):
         return (lax.rem(gx + dx + nx, nx), lax.rem(gy + dy + ny, ny), lax.rem(gz + dz + nz, nz))
 
-    partners = [(0, 0, o) for o in offsets(nz, True)]
-    partners += [(o, 0, 0) for o in offsets(nx) if 1 < o < nx - 1]
-    partners += [(0, o, 0) for o in offsets(ny) if 1 < o < ny - 1]
-    partners += [(dx, dy, 0) for dx, dy in NEAR]
-    barrier = pltpu.get_barrier_semaphore()
-    for p in partners:
-        pl.semaphore_signal(barrier, inc=1, device_id=at(*p), device_id_type=MESH)
-
     loads = [
         pltpu.make_async_copy(source, target, load_sem.at[n])
         for n, (source, target) in enumerate(
@@ -163,7 +155,18 @@
             ]
         )
     ]
-    for load in loads:
+    for load in loads[:2]:
+        load.start()
+
+    partners = [(0, 0, o) for o in offsets(nz, True)]
+    partners += [(o, 0, 0) for o in offsets(nx) if 1 < o < nx - 1]
+    partners += [(0, o, 0) for o in offsets(ny) if 1 < o < ny - 1]
+    partners += [(dx, dy, 0) for dx, dy in NEAR]
+    barrier = pltpu.get_barrier_semaphore()
+    for p in partners:
+        pl.semaphore_signal(barrier, inc=1, device_id=at(*p), device_id_type=MESH)
+
+    for load in loads[2:]:
         load.start()
 
     def remote(src, dst, send, recv, where):

time: 34.2 us -> 34.2 us (level)
  no operation moved by 1% of the time
where the time goes in v7:
time: 34.2 us; the launch traced here: 34 us
  Pallas kernels  33.4 us (98%)
  local copies, waits for them, and re-layouts  0.66 us (2%)
    pallas_call x1, Pallas kernels, local(): pl.pallas_call(functools.partial(kernel, sizes), out_shape=jax.ShapeDtype...  33.4 us

profile of v7, /device:TPU:1, one launch (start us, length us, event | category | flops | bytes accessed | tf_op | source)
XLA Modules:
  0.0 34.0 jit_solution(1605755386034226457)
XLA Ops:
  0.0 33.4 %shard_map.73 = f32[16,16,128]{2,1,0:T(8,128)S(1)} custom-call(f32[16,16,128]{2,1,0:T(8,128)} %charges.1, f32[2,4]{1,0:T(2,128)} %exps_in.1, f32[2,4]{1,0:T(2,128)} %amps_in.1, f32[8,8]{1,0:T(8,128)} %top_x_in.1, f32[8,8]{1,0:T(8,128)} %top_y_in.1, f32[64,64]{1,0:T(8,128)} %top_z_in.1, bf16[592,256]{1,0:T(8,128)(2,1)} %constant.2.clone.table_in), custom_call_target="tpu_custom_call" | custom-call | tf_op jit(solution)/shard_map/pallas_call | solution.py:504
  33.4 0.7 %copy.9 = f32[16,16,128]{2,1,0:T(8,128)} copy(f32[16,16,128]{2,1,0:T(8,128)S(1)} %shard_map.73) | data formatting | bytes 262144
